TPU v7x, 256 devices: a whole 4x4x8 slice. The times are simulated.
256 devices in a mesh: grp: 8 (over y, core), dev: 32 (over z, x).
Axes of the slice: x: 4, y: 4, z: 8, core: 2. Of those that a mesh axis runs over, the one named last changes fastest.
Arguments:
- cell_state: float32 [258, 65536], P(None, ('grp', 'dev')), may hold values from 0.5 to 2, as said below
- stiff_flags: int32 [65536], P(('grp', 'dev')), may hold values from 0 to 1, as said below
- reactants: int32 [2, 1548], replicated, may hold values from 0 to 256, as said below
- collision_frequency_multipliers: float32 [1548], replicated, may hold values from 0.5 to 1.5
- barrier_energies: float32 [1548], replicated, may hold values from 0 to 1
- stoichiometry: float32 [258, 1548], replicated, may hold values from -1 to 1, as said below
- face_cells: int32 [2, 32768], P(None, ('grp', 'dev')), may hold values from 0 to 255
Outputs:
- advanced: float32 [258, 65536], P(None, ('grp', 'dev'))
- face_jump: float32 [258, 2, 32768], P(None, None, ('grp', 'dev'))
Inputs may be any that keep to these rules, and one draw needn't show every extreme that they name: `stiff_flags`: exactly 128 times the number of devices cells are stiff in all; in every draw one device has all 256 of its cells stiff and another none. Both reactants of reaction j lie in block j // 36, that is among components 6 * (j // 36) to 6 * (j // 36) + 5, and are never the temperature, component 258 - 1. `cell_state`: components 0 to 256 lie in [0.5, 1]; component 258 - 1 lies in [1, 2]. `stoichiometry`: every entry has magnitude 0.5 to 1.
All inputs are finite; a program needn't handle non-finite values.
Results may differ from a plain program's by a relative error of at most 0.00023.
Values sent between devices are 32-bit elements; how exact they have to be, the bound alone decides.
A program may use at most 64 MiB of HBM per device.

v0:
```python
import jax
import jax.numpy as jnp
from jax import lax
from jax.sharding import PartitionSpec as P

NB = 43
BS = 6
RPB = 36


TIME_STEP = 0.01
SECTION_GAMMA = 0.5
SECTION_A = (2.0, 1.867943637803922, 0.2344449711399156)
SECTION_C = (
    -7.13761503641231,
    2.580708087951457,
    0.6515950076447975,
    -2.137148994382534,
    -0.3214669691237626,
    -0.6949742501781779,
)
SECTION_M = (2.255570073418735, 0.2870493262186792, 0.435317943184018, 1.093502252409163)


def with_halo(shard, sides, width):
    for axis, dim in sides:
        size, length = (lax.axis_size(axis), shard.shape[dim])
        up = [(i, (i + 1) % size) for i in range(size - 1)]
        down = [(j, i) for i, j in up]
        last = lax.slice_in_dim(shard, length - width, length, axis=dim)
        first = lax.slice_in_dim(shard, 0, width, axis=dim)
        before = lax.ppermute(last, axis, up)
        after = lax.ppermute(first, axis, down)
        shard = jnp.concatenate([before, shard, after], axis=dim)
    return shard


def reaction_speed_constants(zone_thermal_level, collision_frequency_multipliers, barrier_energies):
    return collision_frequency_multipliers[:, None] * jnp.exp(
        barrier_energies[:, None] * (1.0 - 1.0 / zone_thermal_level[None, :])
    )


def mass_action(cell_state, reactants, coefficients):
    former = jnp.take(cell_state, reactants[0], axis=0)
    latter = jnp.take(cell_state, reactants[1], axis=0)
    return coefficients * former * latter


def source_term(stoichiometry, reaction_rates):
    return jnp.dot(
        stoichiometry,
        reaction_rates,
        precision=lax.Precision.HIGHEST,
        preferred_element_type=jnp.float32,
    )


def explicit_step(
    cell_state, reactants, collision_frequency_multipliers, barrier_energies, stoichiometry
):
    coefficients = reaction_speed_constants(
        cell_state[-1], collision_frequency_multipliers, barrier_energies
    )
    return cell_state + TIME_STEP * source_term(
        stoichiometry, mass_action(cell_state, reactants, coefficients)
    )


def block_coupling(stoichiometry, reactants):
    shaped = stoichiometry.reshape(NB, BS, NB, RPB)
    blocks = jnp.transpose(jnp.diagonal(shaped, axis1=0, axis2=2), (2, 0, 1))
    offsets = reactants.reshape(2, NB, RPB) - (jnp.arange(NB, dtype=jnp.int32) * BS)[None, :, None]
    select = (offsets[..., None] == jnp.arange(BS, dtype=jnp.int32)[None, None, None, :]).astype(
        jnp.float32
    )
    by_first = blocks[:, :, None, :] * jnp.transpose(select[0], (0, 2, 1))[:, None, :, :]
    by_second = blocks[:, :, None, :] * jnp.transpose(select[1], (0, 2, 1))[:, None, :, :]
    return jnp.concatenate([by_first, by_second], axis=3).reshape(NB, BS * BS, 2 * RPB)


def factor_blocks(system):
    shaped = system.reshape(NB, BS, BS, -1)
    entries = [[shaped[:, target, column] for column in range(BS)] for target in range(BS)]
    inverses = []
    for pivot_at in range(BS):
        inverse = 1.0 / entries[pivot_at][pivot_at]
        inverses.append(inverse)
        for target in range(pivot_at + 1, BS):
            entries[target][pivot_at] = entries[target][pivot_at] * inverse
            for column in range(pivot_at + 1, BS):
                entries[target][column] = (
                    entries[target][column] - entries[target][pivot_at] * entries[pivot_at][column]
                )
    return (entries, inverses)


def solve_blocks(entries, inverses, right_side):
    blocked = right_side.reshape(NB, BS, -1)
    solution = [blocked[:, target] for target in range(BS)]
    for target in range(BS):
        for column in range(target):
            solution[target] = solution[target] - entries[target][column] * solution[column]
    for target in reversed(range(BS)):
        for column in range(target + 1, BS):
            solution[target] = solution[target] - entries[target][column] * solution[column]
        solution[target] = solution[target] * inverses[target]
    return jnp.stack(solution, axis=1).reshape(NB * BS, -1)


def integrate(
    cell_state,
    reactants,
    collision_frequency_multipliers,
    barrier_energies,
    stoichiometry,
    coupling,
):
    column_count = cell_state.shape[1]
    coefficients = reaction_speed_constants(
        cell_state[-1], collision_frequency_multipliers, barrier_energies
    )
    former = jnp.take(cell_state, reactants[0], axis=0)
    latter = jnp.take(cell_state, reactants[1], axis=0)
    initial = source_term(stoichiometry, coefficients * former * latter)
    factors = jnp.concatenate(
        [
            (coefficients * latter).reshape(NB, RPB, column_count),
            (coefficients * former).reshape(NB, RPB, column_count),
        ],
        axis=1,
    )
    jacobian = jnp.einsum("bkj,bjn->bkn", coupling, factors, precision=lax.Precision.HIGHEST)
    scaled = TIME_STEP * SECTION_GAMMA
    identity = jnp.eye(BS, dtype=jnp.float32).reshape(1, BS * BS, 1)
    entries, inverses = factor_blocks(identity - scaled * jacobian)
    section_one = solve_blocks(entries, inverses, scaled * initial)
    second_state = cell_state + SECTION_A[0] * section_one
    second_rate = source_term(stoichiometry, mass_action(second_state, reactants, coefficients))
    section_two = solve_blocks(
        entries, inverses, scaled * second_rate + SECTION_GAMMA * SECTION_C[0] * section_one
    )
    third_state = cell_state + SECTION_A[1] * section_one + SECTION_A[2] * section_two
    third_rate = source_term(stoichiometry, mass_action(third_state, reactants, coefficients))
    section_three = solve_blocks(
        entries,
        inverses,
        scaled * third_rate
        + SECTION_GAMMA * (SECTION_C[1] * section_one + SECTION_C[2] * section_two),
    )
    section_four = solve_blocks(
        entries,
        inverses,
        scaled * third_rate
        + SECTION_GAMMA
        * (SECTION_C[3] * section_one + SECTION_C[4] * section_two + SECTION_C[5] * section_three),
    )
    return (
        cell_state
        + SECTION_M[0] * section_one
        + SECTION_M[1] * section_two
        + SECTION_M[2] * section_three
        + SECTION_M[3] * section_four
    )


def on_device(
    cell_state,
    stiff_flags,
    reactants,
    collision_frequency_multipliers,
    barrier_energies,
    stoichiometry,
    face_cells,
):
    components = cell_state.shape[0]
    column_count = cell_state.shape[1]
    coupling = block_coupling(stoichiometry, reactants)
    explicit = explicit_step(
        cell_state, reactants, collision_frequency_multipliers, barrier_energies, stoichiometry
    )
    processor_count = lax.axis_size(("grp", "dev"))
    groups = lax.axis_size("grp")
    members = lax.axis_size("dev")
    my_index = lax.axis_index(("grp", "dev"))
    per_pair = -(-column_count // processor_count)
    workload = column_count // 2
    stiff_count = jnp.sum(stiff_flags).reshape(1)
    counts = lax.all_gather(stiff_count, ("grp", "dev"), axis=0, tiled=True)
    offsets = jnp.cumsum(counts) - counts
    range_ends = offsets + counts
    my_offset = offsets[my_index]
    listed = jnp.nonzero(stiff_flags, size=column_count, fill_value=0)[0].astype(jnp.int32)
    slot_order = jnp.arange(processor_count * per_pair, dtype=jnp.int32)
    destination = slot_order // per_pair
    slot_depth = slot_order % per_pair
    local_rank = slot_depth * processor_count + (destination - my_offset) % processor_count
    present = local_rank < stiff_count[0]
    picked = jnp.take(listed, jnp.minimum(local_rank, column_count - 1))
    outgoing = jnp.where(present[None, :], jnp.take(cell_state, picked, axis=1), 0.0)
    outgoing = outgoing.reshape(components, groups, members * per_pair)
    incoming = lax.all_to_all(
        lax.all_to_all(outgoing, "grp", split_axis=1, concat_axis=1, tiled=True),
        "dev",
        split_axis=2,
        concat_axis=2,
        tiled=True,
    )
    incoming = incoming.reshape(components, processor_count * per_pair)
    global_rank = jnp.arange(workload, dtype=jnp.int32) * processor_count + my_index
    source = jnp.sum((range_ends[None, :] <= global_rank[:, None]).astype(jnp.int32), axis=1)
    within = global_rank - jnp.take(offsets, source)
    take_rows = source * per_pair + within // processor_count
    work_cells = jnp.take(incoming, take_rows, axis=1)
    solved = integrate(
        work_cells,
        reactants,
        collision_frequency_multipliers,
        barrier_energies,
        stoichiometry,
        coupling,
    )
    sender_offset = jnp.take(offsets, destination)
    back_rank = slot_depth * processor_count + (my_index - sender_offset) % processor_count
    back_present = back_rank < jnp.take(counts, destination)
    back_slot = jnp.minimum((sender_offset + back_rank) // processor_count, workload - 1)
    returning = jnp.where(back_present[None, :], jnp.take(solved, back_slot, axis=1), 0.0)
    returning = returning.reshape(components, groups, members * per_pair)
    returned = lax.all_to_all(
        lax.all_to_all(returning, "grp", split_axis=1, concat_axis=1, tiled=True),
        "dev",
        split_axis=2,
        concat_axis=2,
        tiled=True,
    )
    returned = returned.reshape(components, processor_count * per_pair)
    home_rank = jnp.maximum(jnp.cumsum(stiff_flags) - 1, 0)
    worker = (my_offset + home_rank) % processor_count
    solved_home = jnp.take(returned, worker * per_pair + home_rank // processor_count, axis=1)
    advanced = jnp.where(stiff_flags[None, :] == 1, solved_home, explicit)
    face_states = jnp.take(advanced, face_cells, axis=1)
    padded = with_halo(face_states, (("dev", 1),), 1)
    face_jump = jnp.stack(
        [padded[:, 0] - face_states[:, 0], padded[:, 3] - face_states[:, 1]], axis=1
    )
    return (advanced, face_jump)


def solution(mesh):
    in_specs = (
        P(None, ("grp", "dev")),
        P(("grp", "dev")),
        P(),
        P(),
        P(),
        P(),
        P(None, ("grp", "dev")),
    )
    out_specs = (P(None, ("grp", "dev")), P(None, None, ("grp", "dev")))
    return jax.shard_map(
        on_device, mesh=mesh, in_specs=in_specs, out_specs=out_specs, check_vma=False
    )
```

profile of v0, /device:TPU:14, one launch (start us, length us, event | category | flops | bytes accessed | tf_op | source)
XLA Modules:
  0.0 281.1 jit_solution(12979487719853236568)
XLA Ops:
  3.9 78.5 %all-reduce = s32[256]{0:T(256)S(1)} all-reduce(s32[256]{0:T(256)S(1)} %dynamic-update-slice), channel_id=1, replica_groups=mesh['grp'=8,'dev'=32] {'grp','dev'}, use_global_device_ids=true, to_apply=%add | all-reduce | flops 256 | bytes 2048
  97.0 5.0 %all-to-all-start = ((f32[258,8,32]{0,2,1:T(8,128)}), f32[258,8,32]{0,2,1:T(8,128)}, u32[]{:S(2)}, u32[]{:S(2)}) async-start(f32[258,8,32]{0,2,1:T(8,128)} %bitcast.16), calls=%async_computation | async-start | bytes 786432 | tf_op jit(solution)/shard_map/all_to_all | solution.py:203
  108.6 6.6 %reshape.3195 = f32[43,6,43,36]{3,2,1,0:T(8,128)} reshape(f32[258,1548]{1,0:T(8,128)S(1)} %copy-done.1) | data formatting | bytes 3195072 | tf_op jit(solution)/shard_map/reshape | solution.py:71
  115.2 8.1 %copy.812 = f32[43,6,43,36]{3,1,2,0:T(8,128)} copy(f32[43,6,43,36]{3,2,1,0:T(8,128)} %reshape.3195) | data formatting | bytes 3195072 | tf_op jit(solution)/shard_map/reshape | solution.py:71
  123.3 3.9 %gather_fusion.2 = f32[43,6,36]{2,1,0:T(8,128)S(1)} fusion(f32[6,36,43,43]{1,0,3,2:T(8,128)} %bitcast.492, s32[43]{0:T(128)S(1)} %or_bitcast_fusion), kind=kCustom, calls=%fused_computation.15 | custom fusion | bytes 74648 | tf_op jit(solution)/shard_map/jit(diagonal)/gather | solution.py:72
  134.6 8.1 %all-to-all-start.1 = ((f32[258,8,32]{0,1,2:T(8,128)}), f32[258,8,32]{0,1,2:T(8,128)S(1)}, u32[]{:S(2)}, u32[]{:S(2)}) async-start(f32[258,8,32]{0,1,2:T(8,128)} %copy.377), calls=%async_computation.1 | async-start | bytes 786432 | tf_op jit(solution)/shard_map/all_to_all | solution.py:202
  143.3 13.6 %all-to-all-done.1 = f32[258,8,32]{0,1,2:T(8,128)S(1)} async-done(((f32[258,8,32]{0,1,2:T(8,128)}), f32[258,8,32]{0,1,2:T(8,128)S(1)}, u32[]{:S(2)}, u32[]{:S(2)}) %all-to-all-start.1) | async-done | bytes 264224 | tf_op jit(solution)/shard_map/all_to_all | solution.py:202
  157.9 4.1 %gather_fusion.9 = f32[1548,128]{1,0:T(8,128)} fusion(f32[258,128]{1,0:T(8,128)S(1)} %select_bitcast_fusion.1, s32[2048]{0:T(1024)S(1)} %pad_clamp_fusion.1), kind=kCustom, calls=%fused_computation.2.clone | custom fusion | bytes 1591344 | tf_op jit(solution)/shard_map/jit(_take)/gather | solution.py:123
  165.3 3.7 %fusion.30 = (f32[1548,128]{1,0:T(8,128)}, f32[1548,128]{1,0:T(8,128)S(1)}) fusion(f32[1548,128]{1,0:T(8,128)S(1)} %gather_fusion.10, f32[128]{0:T(128)S(1)} %fusion.156, f32[1548]{0:T(1024)S(1)} %copy-done.50, f32[1548]{0:T(1024)S(1)} %copy-done.52, pred[1548]{0:T(1024)(128)(4,1)S(1)} %get-tuple-element.151, f32[1548,128]{1,0:T(8,128)} %gather_fusion.9, ...), kind=kLoop, calls=%fused_computation.57 | loop fusion | flops 1188864 | bytes 3186296 | tf_op jit(solution)/shard_map/mul | solution.py:128
  172.1 3.7 %fusion.11 = f32[43,36,128]{2,1,0:T(8,128)S(1)} fusion(f32[43,36,128]{2,1,0:T(8,128)} %reshape.3198, f32[43,36,128]{2,1,0:T(8,128)} %reshape.3197, f32[43,36,36]{2,1,0:T(8,128)} %copy.384, f32[43,36,36]{2,1,0:T(8,128)} %copy.383, f32[36]{0:T(128)S(1)} %reshape.3206), kind=kOutput, calls=%fused_computation.31 | convolution fusion | flops 172100448 | bytes 2823696 | tf_op jit(solution)/shard_map/bkj,bjn->bkn/dot_general | solution.py:133
  185.8 3.2 %gather_fusion.11 = f32[1548,128]{1,0:T(8,128)S(1)} fusion(f32[258,128]{1,0:T(8,128)S(1)} %fusion.210, s32[2048]{0:T(1024)S(1)} %copy-done.46), kind=kCustom, calls=%fused_computation.8.clone | custom fusion | bytes 1591344 | tf_op jit(solution)/shard_map/jit(_take)/gather | solution.py:45
  189.1 4.2 %gather_fusion.12 = f32[1548,128]{1,0:T(8,128)} fusion(f32[258,128]{1,0:T(8,128)S(1)} %fusion.210, s32[2048]{0:T(1024)S(1)} %copy-done.48), kind=kCustom, calls=%fused_computation.9.clone | custom fusion | bytes 1591344 | tf_op jit(solution)/shard_map/jit(_take)/gather | solution.py:46
  194.0 4.3 %fusion.20 = f32[258,128]{1,0:T(8,128)} fusion(f32[258,128]{1,0:T(8,128)} %mul.4862, f32[258,1548]{1,0:T(8,128)S(1)} %copy-done.1, f32[1548,128]{1,0:T(8,128)} %gather_fusion.12, f32[1548,128]{1,0:T(8,128)S(1)} %gather_fusion.11, f32[128]{0:T(128)} %copy-done.65, f32[1548]{0:T(1024)} %param.19, f32[1548]{0:T(1024)} %param.18, ...), kind=kOutput, calls=%fused_computation.40 | convolution fusion | flops 614708736 | bytes 3462872 | tf_op jit(solution)/shard_map/dot_general | solution.py:51
  201.3 3.4 %gather_fusion.13 = f32[1548,128]{1,0:T(8,128)S(1)} fusion(f32[258,128]{1,0:T(8,128)S(1)} %add_add_fusion.1, s32[2048]{0:T(1024)S(1)} %copy-done.46), kind=kCustom, calls=%fused_computation.10.clone | custom fusion | bytes 1591344 | tf_op jit(solution)/shard_map/jit(_take)/gather | solution.py:45
  204.6 4.6 %gather_fusion.14 = f32[1548,128]{1,0:T(8,128)} fusion(f32[258,128]{1,0:T(8,128)S(1)} %add_add_fusion.1, s32[2048]{0:T(1024)} %copy-done.47), kind=kCustom, calls=%fused_computation.11.clone | custom fusion | bytes 1591344 | tf_op jit(solution)/shard_map/jit(_take)/gather | solution.py:46
  209.9 4.3 %fusion.205 = (f32[258,128]{1,0:T(8,128)}, f32[258,128]{1,0:T(8,128)}) fusion(f32[258,128]{1,0:T(8,128)} %mul.4917, f32[258,1548]{1,0:T(8,128)S(1)} %copy-done.1, f32[1548,128]{1,0:T(8,128)} %gather_fusion.14, f32[1548,128]{1,0:T(8,128)S(1)} %gather_fusion.13, f32[128]{0:T(128)} %copy-done.65, f32[1548]{0:T(1024)} %param.19, f32[1548]{0:T(1024)} %param.18, ...), kind=kOutput, calls=%fused_computation.391 | convolution fusion | flops 614708736 | bytes 3594968 | tf_op jit(solution)/shard_map/dot_general | solution.py:51
  223.2 4.8 %all-to-all-start.2 = ((f32[258,8,32]{0,2,1:T(8,128)}), f32[258,8,32]{0,2,1:T(8,128)S(1)}, u32[]{:S(2)}, u32[]{:S(2)}) async-start(f32[258,8,32]{0,2,1:T(8,128)} %select_select_fusion), calls=%async_computation.2 | async-start | bytes 786432 | tf_op jit(solution)/shard_map/all_to_all | solution.py:230
  228.1 5.2 %gather_fusion.16 = f32[1548,256]{1,0:T(8,128)} fusion(f32[258,256]{1,0:T(8,128)S(1)} %copy-done, s32[2048]{0:T(1024)S(1)} %copy-done.46), kind=kCustom, calls=%fused_computation.3.clone | custom fusion | bytes 3176496 | tf_op jit(solution)/shard_map/jit(_take)/gather | solution.py:45
  233.3 5.2 %gather_fusion.17 = f32[1548,256]{1,0:T(8,128)} fusion(f32[258,256]{1,0:T(8,128)S(1)} %copy-done, s32[2048]{0:T(1024)S(1)} %copy-done.49), kind=kCustom, calls=%fused_computation.12.clone | custom fusion | bytes 3176496 | tf_op jit(solution)/shard_map/jit(_take)/gather | solution.py:46
  239.4 5.6 %all-to-all-start.3 = ((f32[258,8,32]{0,1,2:T(8,128)}), f32[258,8,32]{0,1,2:T(8,128)S(1)}, u32[]{:S(2)}, u32[]{:S(2)}) async-start(f32[258,8,32]{0,1,2:T(8,128)} %copy.423), calls=%async_computation.3 | async-start | bytes 786432 | tf_op jit(solution)/shard_map/all_to_all | solution.py:229
  245.1 14.3 %all-to-all-done.3 = f32[258,8,32]{0,1,2:T(8,128)S(1)} async-done(((f32[258,8,32]{0,1,2:T(8,128)}), f32[258,8,32]{0,1,2:T(8,128)S(1)}, u32[]{:S(2)}, u32[]{:S(2)}) %all-to-all-start.3) | async-done | bytes 264224 | tf_op jit(solution)/shard_map/all_to_all | solution.py:229
  260.7 4.2 %fusion.17 = f32[258,256]{1,0:T(8,128)S(1)} fusion(f32[258,256]{1,0:T(8,128)S(1)} %copy-done, f32[258,1548]{1,0:T(8,128)S(1)} %copy-done.1, f32[1548,256]{1,0:T(8,128)} %gather_fusion.17, f32[1548,256]{1,0:T(8,128)} %gather_fusion.16, f32[256]{0:T(256)S(1)} %bitcast.502, f32[1548]{0:T(1024)S(1)} %copy-done.51, f32[1548]{0:T(1024)S(1)} %copy-done.53, ...), kind=kOutput, calls=%fused_computation.35 | convolution fusion | flops 1229549568 | bytes 5577432 | tf_op jit(solution)/shard_map/dot_general | solution.py:51
  266.6 4.0 %collective-permute-start = (f32[258,1,128]{2,1,0:T(1,128)S(1)}, f32[258,1,128]{2,1,0:T(1,128)S(1)}, u32[]{:S(2)}, u32[]{:S(2)}) collective-permute-start(f32[258,1,128]{2,1,0:T(1,128)S(1)} %get-tuple-element.128), channel_id=1, source_target_pairs={{0,1},{1,2},{2,3},{3,4},{4,5},{5,6},{6,7},{7,8},{8,9},{9,10},{10,1... | collective-permute-start | bytes 396296 | tf_op jit(solution)/shard_map/ppermute | solution.py:32
  273.5 6.2 %collective-permute-done.1 = f32[258,1,128]{2,1,0:T(1,128)S(1)} collective-permute-done((f32[258,1,128]{2,1,0:T(1,128)S(1)}, f32[258,1,128]{2,1,0:T(1,128)S(1)}, u32[]{:S(2)}, u32[]{:S(2)}) %collective-permute-start.1) | collective-permute-done | bytes 132128 | tf_op jit(solution)/shard_map/ppermute | solution.py:33
  (285 shorter events, 70.0 us)
Async XLA Ops:
  95.1 7.0 %copy-start.58 = (s32[2,1548]{1,0:T(2,128)S(1)}, s32[2,1548]{1,0:T(2,128)}, u32[]{:S(2)}) copy-start(s32[2,1548]{1,0:T(2,128)} %param.17) | copy-start | bytes 37156
  97.0 35.6 %all-to-all-start = ((f32[258,8,32]{0,2,1:T(8,128)}), f32[258,8,32]{0,2,1:T(8,128)}, u32[]{:S(2)}, u32[]{:S(2)}) async-start(f32[258,8,32]{0,2,1:T(8,128)} %bitcast.16), calls=%async_computation | async-start | bytes 786432 | tf_op jit(solution)/shard_map/all_to_all | solution.py:203
  102.3 6.3 %copy-start.1 = (f32[258,1548]{1,0:T(8,128)S(1)}, f32[258,1548]{1,0:T(8,128)}, u32[]{:S(2)}) copy-start(f32[258,1548]{1,0:T(8,128)} %param.20) | copy-start | bytes 4792612
  132.5 25.3 %copy-start.45 = (s32[2048]{0:T(1024)}, s32[2048]{0:T(1024)S(1)}, u32[]{:S(2)}) copy-start(s32[2048]{0:T(1024)S(1)} %pad_clamp_fusion.1) | copy-start | bytes 24580
  132.6 29.5 %copy-start.47 = (s32[2048]{0:T(1024)}, s32[2048]{0:T(1024)S(1)}, u32[]{:S(2)}) copy-start(s32[2048]{0:T(1024)S(1)} %pad_clamp_fusion) | copy-start | bytes 24580
  134.6 22.3 %all-to-all-start.1 = ((f32[258,8,32]{0,1,2:T(8,128)}), f32[258,8,32]{0,1,2:T(8,128)S(1)}, u32[]{:S(2)}, u32[]{:S(2)}) async-start(f32[258,8,32]{0,1,2:T(8,128)} %copy.377), calls=%async_computation.1 | async-start | bytes 786432 | tf_op jit(solution)/shard_map/all_to_all | solution.py:202
  143.3 14.6 %copy-start.61 = (pred[128]{0:T(512)(128)(4,1)}, pred[128]{0:T(512)(128)(4,1)S(1)}, u32[]{:S(2)}) copy-start(pred[128]{0:T(512)(128)(4,1)S(1)} %compare_and_fusion.5) | copy-start | bytes 388
  143.3 21.9 %copy-start.54 = (pred[1548]{0:T(1024)(128)(4,1)}, pred[1548]{0:T(1024)(128)(4,1)S(1)}, u32[]{:S(2)}) copy-start(pred[1548]{0:T(1024)(128)(4,1)S(1)} %get-tuple-element.151) | copy-start | bytes 4648
  143.3 21.9 %copy-start.59 = (pred[1548]{0:T(1024)(128)(4,1)}, pred[1548]{0:T(1024)(128)(4,1)S(1)}, u32[]{:S(2)}) copy-start(pred[1548]{0:T(1024)(128)(4,1)S(1)} %get-tuple-element.152) | copy-start | bytes 4648
  157.9 7.3 %copy-start.65 = (f32[128]{0:T(128)}, f32[128]{0:T(128)S(1)}, u32[]{:S(2)}) copy-start(f32[128]{0:T(128)S(1)} %fusion.156) | copy-start | bytes 1540
  182.5 6.5 %copy-start.9 = (f32[43,1,128]{2,1,0:T(1,128)}, f32[43,1,128]{2,1,0:T(1,128)S(1)}, u32[]{:S(2)}) copy-start(f32[43,1,128]{2,1,0:T(1,128)S(1)} %get-tuple-element.73) | copy-start | bytes 66052
  182.5 6.5 %copy-start.13 = (f32[43,1,128]{2,1,0:T(1,128)}, f32[43,1,128]{2,1,0:T(1,128)S(1)}, u32[]{:S(2)}) copy-start(f32[43,1,128]{2,1,0:T(1,128)S(1)} %get-tuple-element.77) | copy-start | bytes 66052
  182.5 16.7 %copy-start.6 = (f32[43,1,128]{2,1,0:T(1,128)}, f32[43,1,128]{2,1,0:T(1,128)S(1)}, u32[]{:S(2)}) copy-start(f32[43,1,128]{2,1,0:T(1,128)S(1)} %get-tuple-element.72) | copy-start | bytes 66052
  193.9 5.5 %copy-start.3 = (f32[43,1,1,128]{3,0,2,1:T(8,128)S(1)}, f32[43,1,1,128]{3,0,2,1:T(8,128)}, u32[]{:S(2)}) copy-start(f32[43,1,1,128]{3,0,2,1:T(8,128)} %get-tuple-element.124) | copy-start | bytes 66052
  194.0 5.5 %copy-start.4 = (f32[43,1,1,128]{3,0,2,1:T(8,128)S(1)}, f32[43,1,1,128]{3,0,2,1:T(8,128)}, u32[]{:S(2)}) copy-start(f32[43,1,1,128]{3,0,2,1:T(8,128)} %get-tuple-element.100) | copy-start | bytes 66052
  194.0 5.5 %copy-start.5 = (f32[43,1,1,128]{3,0,2,1:T(8,128)S(1)}, f32[43,1,1,128]{3,0,2,1:T(8,128)}, u32[]{:S(2)}) copy-start(f32[43,1,1,128]{3,0,2,1:T(8,128)} %get-tuple-element.108) | copy-start | bytes 66052
  194.0 5.5 %copy-start.35 = (f32[43,1,128]{2,1,0:T(1,128)S(1)}, f32[43,1,128]{2,1,0:T(1,128)}, u32[]{:S(2)}) copy-start(f32[43,1,128]{2,1,0:T(1,128)} %copy-done.34) | copy-start | bytes 66052
  194.0 5.5 %copy-start.38 = (f32[43,1,128]{2,1,0:T(1,128)S(1)}, f32[43,1,128]{2,1,0:T(1,128)}, u32[]{:S(2)}) copy-start(f32[43,1,128]{2,1,0:T(1,128)} %copy-done.37) | copy-start | bytes 66052
  221.1 7.0 %copy-start.66 = (s32[256]{0:T(256)S(1)}, s32[256]{0:T(256)}, u32[]{:S(2)}) copy-start(s32[256]{0:T(256)} %get-tuple-element.11) | copy-start | bytes 3076
  221.1 7.0 %copy-start = (f32[258,256]{1,0:T(8,128)S(1)}, f32[258,256]{1,0:T(8,128)}, u32[]{:S(2)}) copy-start(f32[258,256]{1,0:T(8,128)} %param.15) | copy-start | bytes 792580
  223.2 15.2 %all-to-all-start.2 = ((f32[258,8,32]{0,2,1:T(8,128)}), f32[258,8,32]{0,2,1:T(8,128)S(1)}, u32[]{:S(2)}, u32[]{:S(2)}) async-start(f32[258,8,32]{0,2,1:T(8,128)} %select_select_fusion), calls=%async_computation.2 | async-start | bytes 786432 | tf_op jit(solution)/shard_map/all_to_all | solution.py:230
  239.4 19.9 %all-to-all-start.3 = ((f32[258,8,32]{0,1,2:T(8,128)}), f32[258,8,32]{0,1,2:T(8,128)S(1)}, u32[]{:S(2)}, u32[]{:S(2)}) async-start(f32[258,8,32]{0,1,2:T(8,128)} %copy.423), calls=%async_computation.3 | async-start | bytes 786432 | tf_op jit(solution)/shard_map/all_to_all | solution.py:229
  266.6 6.9 %collective-permute-start = (f32[258,1,128]{2,1,0:T(1,128)S(1)}, f32[258,1,128]{2,1,0:T(1,128)S(1)}, u32[]{:S(2)}, u32[]{:S(2)}) collective-permute-start(f32[258,1,128]{2,1,0:T(1,128)S(1)} %get-tuple-element.128), channel_id=1, source_target_pairs={{0,1},{1,2},{2,3},{3,4},{4,5},{5,6},{6,7},{7,8},{8,9},{9,10},{10,1... | collective-permute-start | bytes 396296 | tf_op jit(solution)/shard_map/ppermute | solution.py:32
  270.6 9.0 %collective-permute-start.1 = (f32[258,1,128]{2,1,0:T(1,128)S(1)}, f32[258,1,128]{2,1,0:T(1,128)S(1)}, u32[]{:S(2)}, u32[]{:S(2)}) collective-permute-start(f32[258,1,128]{2,1,0:T(1,128)S(1)} %get-tuple-element.129), channel_id=1, source_target_pairs={{1,0},{2,1},{3,2},{4,3},{5,4},{6,5},{7,6},{8,7},{9,8},{10,9},{11,1... | collective-permute-start | bytes 396296 | tf_op jit(solution)/shard_map/ppermute | solution.py:33
  (54 other events, 184.9 us)
where the time goes:
time: 286 us; the launch traced here: 281 us
  local copies, waits for them, and re-layouts  85.5 us (30%)
  blocking collectives  78.5 us (27%)
  waiting for transfers between devices  34.9 us (12%)
  other arithmetic  31.4 us (11%)
  starting transfers between devices  29.5 us (10%)
  matrix products  18.9 us (7%)
    unnamed x1, blocking collectives  78.5 us
    dot_general x4, matrix products, source_term(): jnp.dot(stoichiometry, reaction_rates, precision=lax.Precision.HIGHEST, p...  15.1 us
    reshape x2, local copies, waits for them, and re-layouts, block_coupling(): shaped = stoichiometry.reshape(NB, BS, NB, RPB)  14.7 us
    all_to_all x1, waiting for transfers between devices, on_device(): lax.all_to_all(lax.all_to_all(returning, 'grp', split_axis=1, concat_axis...  14.3 us
    gather x3, local copies, waits for them, and re-layouts, mass_action(): latter = jnp.take(cell_state, reactants[1], axis=0)  14 us
    all_to_all x1, waiting for transfers between devices, on_device(): lax.all_to_all(lax.all_to_all(outgoing, 'grp', split_axis=1, concat_axis=...  13.6 us
    gather x3, local copies, waits for them, and re-layouts, mass_action(): former = jnp.take(cell_state, reactants[0], axis=0)  11.7 us
    all_to_all x1, starting transfers between devices, on_device(): lax.all_to_all(lax.all_to_all(outgoing, 'grp', split_axis=1, concat_axis=...  8.1 us
  transfers between devices with their start and end apart: 6, of which 4 were waited for; matrix products, arithmetic and copies ran while one was open for 15% of the time, Pallas kernels for 0%

commit v1 on v0

v1 whole, which is shorter than its diff:
```python
import jax
import jax.numpy as jnp
from jax import lax
from jax.experimental import pallas as pl
from jax.experimental.pallas import tpu as pltpu
from jax.sharding import PartitionSpec as P

NB = 43
BS = 6
RPB = 36
SPEC = 258
NR = 1548
CELLS = 256
FACES = 128

GROUP = 8
GROUPS = 6
GROUP_STATE = GROUP * BS
GROUP_RATES = GROUP * RPB
STATE_ROWS = GROUPS * GROUP_STATE
LAST_RATES = 112
RATE_ROWS = 1664
CHUNK = 96
S_ROWS = 272

TIME_STEP = 0.01
GAMMA = 0.5
SCALED = TIME_STEP * GAMMA
A = (2.0, 1.867943637803922, 0.2344449711399156)
C = (
    -7.13761503641231,
    2.580708087951457,
    0.6515950076447975,
    -2.137148994382534,
    -0.3214669691237626,
    -0.6949742501781779,
)
M = (2.255570073418735, 0.2870493262186792, 0.435317943184018, 1.093502252409163)

BF = jnp.bfloat16
F32 = jnp.float32


def dot(a, b):
    return jnp.dot(a, b, preferred_element_type=F32)


def split2(x):
    hi = x.astype(BF)
    return hi, (x - hi.astype(F32)).astype(BF)


def split3(x):
    hi = x.astype(BF)
    rest = x - hi.astype(F32)
    mid = rest.astype(BF)
    return hi, mid, (rest - mid.astype(F32)).astype(BF)


def chunks_of(group):
    start = group * GROUP_RATES
    if group == GROUPS - 1:
        return [(start, LAST_RATES)]
    return [(start + k, CHUNK) for k in range(0, GROUP_RATES, CHUNK)]


def window_of(group):
    start = group * GROUP_RATES // 128 * 128
    return start, (256 if group == GROUPS - 1 else 384)


def factor(e):
    for p in range(BS):
        inverse = 1.0 / e[p][p]
        e[p][p] = inverse
        for t in range(p + 1, BS):
            e[t][p] = e[t][p] * inverse
            for c in range(p + 1, BS):
                e[t][c] = e[t][c] - e[t][p] * e[p][c]
    return e


def solve(e, b):
    x = list(b)
    for t in range(BS):
        for c in range(t):
            x[t] = x[t] - e[t][c] * x[c]
    for t in reversed(range(BS)):
        for c in range(t + 1, BS):
            x[t] = x[t] - e[t][c] * x[c]
        x[t] = x[t] * e[t][t]
    return x


def kernel(
    state_ref,
    flags_ref,
    reactants_ref,
    frequency_ref,
    barrier_ref,
    stoich_ref,
    faces_ref,
    advanced_ref,
    face_ref,
    rows,
    columns,
    s_hi,
    s_lo,
    s_tile,
    y_half,
    src_half,
    y0,
    gather,
    y_split,
    coef,
    r_hi,
    r_lo,
    fac,
    coupling,
    lu,
    explicit,
    u1,
    u2,
):
    rows[...] = jnp.zeros_like(rows)
    rows[:, 1536:] = jnp.where(
        lax.broadcasted_iota(jnp.int32, (8, 128), 0) >= 2, -1.0, 0.0
    )
    rows[0:1, :NR] = frequency_ref[...]
    rows[1:2, :NR] = barrier_ref[...]
    reactants = reactants_ref[...]
    lane = lax.broadcasted_iota(jnp.int32, (2, NR), 1)
    first = jnp.zeros((2, NR), jnp.int32)
    for g in range(1, GROUPS):
        first = jnp.where(lane >= g * GROUP_RATES, g * GROUP_STATE, first)
    local = reactants - first
    block = (local * 43) >> 8
    slot = (local - block * BS) * GROUP + block
    rows[2:4, :NR] = slot.astype(F32)
    rows[4:6, :NR] = reactants.astype(F32)
    columns[...] = jnp.transpose(rows[...])

    y_half[:, SPEC // 8 * 8 :, :] = jnp.zeros((2, STATE_ROWS - SPEC // 8 * 8, 128), F32)
    src_half[:, SPEC // 8 * 8 :, :] = jnp.zeros((2, STATE_ROWS - SPEC // 8 * 8, 128), F32)
    for h in range(2):
        y_half[h, :SPEC, :] = state_ref[:, h * 128 : (h + 1) * 128]
    s_hi[:, 1536:] = jnp.zeros((S_ROWS, 128), BF)
    s_lo[:, 1536:] = jnp.zeros((S_ROWS, 128), BF)
    s_hi[256:, :] = jnp.zeros((S_ROWS - 256, RATE_ROWS), BF)
    s_lo[256:, :] = jnp.zeros((S_ROWS - 256, RATE_ROWS), BF)
    for at in range(0, SPEC, 16):
        n = min(16, SPEC - at)
        hi, lo = split2(stoich_ref[at : at + n, :])
        s_hi[at : at + n, :NR] = hi
        s_lo[at : at + n, :NR] = lo

    for g in range(GROUPS):
        for start, n in chunks_of(g):
            spot = lax.rem(lax.broadcasted_iota(jnp.int32, (n, 3 * GROUP_STATE), 1), GROUP_STATE)
            for which in range(2):
                want = columns[start : start + n, 2 + which : 3 + which].astype(jnp.int32)
                hot = (want == spot).astype(F32).astype(BF)
                gather[which, start : start + n, :] = hot

    def spread(ref, g, h):
        return [ref[h, pl.ds(g * GROUP_STATE + m, GROUP, stride=BS), :] for m in range(BS)]

    def pieces(ref, g, h):
        at = g * GROUP_STATE
        lanes = slice(h * 128, (h + 1) * 128)
        return [ref[at + m * GROUP : at + (m + 1) * GROUP, lanes] for m in range(BS)]

    def put(ref, g, h, values):
        at = g * GROUP_STATE
        lanes = slice(h * 128, (h + 1) * 128)
        for m in range(BS):
            ref[at + m * GROUP : at + (m + 1) * GROUP, lanes] = values[m]

    def put_state(g, parts):
        for k, part in enumerate(split3(parts)):
            at = g * 3 * GROUP_STATE + k * GROUP_STATE
            y_split[at : at + GROUP_STATE, :] = part

    def reactant(which, g, start, n):
        at = g * 3 * GROUP_STATE
        return dot(gather[which, start : start + n, :], y_split[at : at + 3 * GROUP_STATE, :])

    r_hi[NR // 16 * 16 :, :] = jnp.zeros((RATE_ROWS - NR // 16 * 16, CELLS), BF)
    r_lo[NR // 16 * 16 :, :] = jnp.zeros((RATE_ROWS - NR // 16 * 16, CELLS), BF)
    fac[:, NR // 16 * 16 :, :] = jnp.zeros((2, RATE_ROWS - NR // 16 * 16, CELLS), BF)

    theta = 1.0 - 1.0 / state_ref[SPEC - 1 : SPEC, :]
    for g in range(GROUPS):
        for h in range(2):
            put(y0, g, h, spread(y_half, g, h))
        put_state(g, y0[g * GROUP_STATE : (g + 1) * GROUP_STATE, :])
        for start, n in chunks_of(g):
            k = columns[start : start + n, 0:1] * jnp.exp(columns[start : start + n, 1:2] * theta)
            coef[start : start + n, :] = k
            former = reactant(0, g, start, n)
            latter = reactant(1, g, start, n)
            by_first = k * latter
            fac[0, start : start + n, :] = by_first.astype(BF)
            fac[1, start : start + n, :] = (k * former).astype(BF)
            hi, lo = split2(by_first * former)
            r_hi[start : start + n, :] = hi
            r_lo[start : start + n, :] = lo

    def source_term():
        total = (
            dot(s_hi[...], r_hi[...]) + dot(s_lo[...], r_hi[...]) + dot(s_hi[...], r_lo[...])
        )
        for h in range(2):
            src_half[h, :S_ROWS, :] = total[:, h * 128 : (h + 1) * 128]

    def rates():
        for g in range(GROUPS):
            for start, n in chunks_of(g):
                k = coef[start : start + n, :]
                hi, lo = split2(k * reactant(0, g, start, n) * reactant(1, g, start, n))
                r_hi[start : start + n, :] = hi
                r_lo[start : start + n, :] = lo

    source_term()

    sub = lax.broadcasted_iota(jnp.int32, (GROUP, 1), 0) * BS
    for g in range(GROUPS):
        w, width = window_of(g)
        rows_here = min(GROUP_STATE, SPEC - g * GROUP_STATE)
        if rows_here < GROUP_STATE:
            s_tile[...] = jnp.zeros_like(s_tile)
        for t in range(0, width, 128):
            last = min(128, NR - w - t)
            if last > 0:
                s_tile[t // 128, :rows_here, :last] = stoich_ref[
                    g * GROUP_STATE : g * GROUP_STATE + rows_here, w + t : w + t + last
                ]
        slabs = [
            [s_tile[t, pl.ds(i, GROUP, stride=BS), :] for t in range(width // 128)]
            for i in range(BS)
        ]
        for which in range(2):
            reacts = rows[4 + which : 5 + which, w : w + width].astype(jnp.int32)
            masks = [reacts == sub + (g * GROUP_STATE + m) for m in range(BS)]
            for i in range(BS):
                s = jnp.concatenate(slabs[i], axis=1)
                for m in range(0, BS, 2):
                    pair = jnp.concatenate(
                        [jnp.where(masks[m], s, 0.0), jnp.where(masks[m + 1], s, 0.0)], axis=0
                    )
                    to = (i * BS + m) * GROUP
                    coupling[to : to + 16, which * width : (which + 1) * width] = pair.astype(BF)
        jacobian = dot(coupling[:, :width], fac[0, w : w + width, :]) + dot(
            coupling[:, width : 2 * width], fac[1, w : w + width, :]
        )
        lu[g, :, :] = jacobian

    def put_split(g, h, values):
        lanes = slice(h * 128, (h + 1) * 128)
        at = g * 3 * GROUP_STATE
        for m in range(0, BS, 2):
            both = jnp.concatenate([values[m], values[m + 1]], axis=0)
            for k, part in enumerate(split3(both)):
                to = at + k * GROUP_STATE + m * GROUP
                y_split[to : to + 16, lanes] = part

    def factors(g, h):
        lanes = slice(h * 128, (h + 1) * 128)
        return [
            [
                lu[g, (i * BS + m) * GROUP : (i * BS + m + 1) * GROUP, lanes]
                for m in range(BS)
            ]
            for i in range(BS)
        ]

    for g in range(GROUPS):
        for h in range(2):
            lanes = slice(h * 128, (h + 1) * 128)
            e = factors(g, h)
            e = [
                [(1.0 if i == m else 0.0) - SCALED * e[i][m] for m in range(BS)]
                for i in range(BS)
            ]
            e = factor(e)
            for i in range(BS):
                for m in range(BS):
                    lu[g, (i * BS + m) * GROUP : (i * BS + m + 1) * GROUP, lanes] = e[i][m]
            x = solve(e, [SCALED * s for s in spread(src_half, g, h)])
            put(u1, g, h, x)
            put_split(g, h, [y + A[0] * u for y, u in zip(pieces(y0, g, h), x)])
            y = pieces(y0, g, h)
            s = spread(src_half, g, h)
            put(explicit, g, h, [a + TIME_STEP * b for a, b in zip(y, s)])

    rates()
    source_term()
    for g in range(GROUPS):
        for h in range(2):
            e = factors(g, h)
            one = pieces(u1, g, h)
            x = solve(
                e, [SCALED * s + (GAMMA * C[0]) * u for s, u in zip(spread(src_half, g, h), one)]
            )
            put(u2, g, h, x)
            put_split(
                g,
                h,
                [y + A[1] * a + A[2] * b for y, a, b in zip(pieces(y0, g, h), one, x)],
            )

    rates()
    source_term()
    hot = jnp.concatenate(
        [
            lax.broadcasted_iota(jnp.int32, (CELLS, FACES), 0) == faces_ref[0:1, :],
            lax.broadcasted_iota(jnp.int32, (CELLS, FACES), 0) == faces_ref[1:2, :],
        ],
        axis=1,
    )
    hot = hot.astype(F32).astype(BF)
    for g in range(GROUPS):
        for h in range(2):
            lanes = slice(h * 128, (h + 1) * 128)
            e = factors(g, h)
            one = pieces(u1, g, h)
            two = pieces(u2, g, h)
            base = [SCALED * s for s in spread(src_half, g, h)]
            three = solve(
                e,
                [
                    s + (GAMMA * C[1]) * a + (GAMMA * C[2]) * b
                    for s, a, b in zip(base, one, two)
                ],
            )
            four = solve(
                e,
                [
                    s + (GAMMA * C[3]) * a + (GAMMA * C[4]) * b + (GAMMA * C[5]) * c
                    for s, a, b, c in zip(base, one, two, three)
                ],
            )
            stiff = flags_ref[0:1, lanes] == 1
            out = [
                jnp.where(stiff, y + M[0] * a + M[1] * b + M[2] * c + M[3] * d, x)
                for y, a, b, c, d, x in zip(
                    pieces(y0, g, h), one, two, three, four, pieces(explicit, g, h)
                )
            ]
            for m in range(BS):
                y_half[h, pl.ds(g * GROUP_STATE + m, GROUP, stride=BS), :] = out[m]
        count = min(GROUP_STATE, SPEC - g * GROUP_STATE)
        here = slice(g * GROUP_STATE, g * GROUP_STATE + GROUP_STATE)
        real = slice(g * GROUP_STATE, g * GROUP_STATE + count)
        done = jnp.concatenate([y_half[0, here, :], y_half[1, here, :]], axis=1)
        advanced_ref[real, :] = done[:count]
        face = sum(dot(part, hot) for part in split3(done))
        face_ref[real, :] = face[:count]


def compute(state, flags, reactants, frequency, barrier, stoich, faces):
    return pl.pallas_call(
        kernel,
        out_shape=(
            jax.ShapeDtypeStruct((SPEC, CELLS), F32),
            jax.ShapeDtypeStruct((SPEC, 2 * FACES), F32),
        ),
        in_specs=[pl.BlockSpec(memory_space=pltpu.VMEM)] * 7,
        out_specs=[pl.BlockSpec(memory_space=pltpu.VMEM)] * 2,
        scratch_shapes=[
            pltpu.VMEM((8, RATE_ROWS), F32),
            pltpu.VMEM((RATE_ROWS, 8), F32),
            pltpu.VMEM((S_ROWS, RATE_ROWS), BF),
            pltpu.VMEM((S_ROWS, RATE_ROWS), BF),
            pltpu.VMEM((3, GROUP_STATE, 128), F32),
            pltpu.VMEM((2, STATE_ROWS, 128), F32),
            pltpu.VMEM((2, STATE_ROWS, 128), F32),
            pltpu.VMEM((STATE_ROWS, CELLS), F32),
            pltpu.VMEM((2, RATE_ROWS, 3 * GROUP_STATE), BF),
            pltpu.VMEM((3 * STATE_ROWS, CELLS), BF),
            pltpu.VMEM((RATE_ROWS, CELLS), F32),
            pltpu.VMEM((RATE_ROWS, CELLS), BF),
            pltpu.VMEM((RATE_ROWS, CELLS), BF),
            pltpu.VMEM((2, RATE_ROWS, CELLS), BF),
            pltpu.VMEM((STATE_ROWS, 768), BF),
            pltpu.VMEM((GROUPS, STATE_ROWS, CELLS), F32),
            pltpu.VMEM((STATE_ROWS, CELLS), F32),
            pltpu.VMEM((STATE_ROWS, CELLS), F32),
            pltpu.VMEM((STATE_ROWS, CELLS), F32),
        ],
        compiler_params=pltpu.CompilerParams(vmem_limit_bytes=48 * 1024 * 1024),
        cost_estimate=pl.CostEstimate(
            flops=4_000_000_000, bytes_accessed=3_000_000, transcendentals=400_000
        ),
    )(
        state,
        flags.reshape(1, CELLS),
        reactants,
        frequency.reshape(1, NR),
        barrier.reshape(1, NR),
        stoich,
        faces,
    )


def on_device(state, flags, reactants, frequency, barrier, stoich, faces):
    advanced, face = compute(state, flags, reactants, frequency, barrier, stoich, faces)
    lower, upper = face[:, :FACES], face[:, FACES:]
    size = lax.axis_size("dev")
    up = [(i, i + 1) for i in range(size - 1)]
    down = [(i + 1, i) for i in range(size - 1)]
    before = lax.ppermute(upper, "dev", up)
    after = lax.ppermute(lower, "dev", down)
    return advanced, jnp.stack([before - lower, after - upper], axis=1)


def solution(mesh):
    cells = P(None, ("grp", "dev"))
    return jax.shard_map(
        on_device,
        mesh=mesh,
        in_specs=(cells, P(("grp", "dev")), P(), P(), P(), P(), cells),
        out_specs=(cells, P(None, None, ("grp", "dev"))),
        check_vma=False,
    )
```

time: 286 us -> 32.6 us (0.11)
  the two profiles are of different devices: /device:TPU:14 before, /device:TPU:126 now
where the time goes in v1:
time: 32.6 us; the launch traced here: 32.2 us
  Pallas kernels  9.51 us (29%)
  waiting for transfers between devices  8.33 us (26%)
  starting transfers between devices  6.87 us (21%)
  local copies, waits for them, and re-layouts  6.75 us (21%)
  between operations  0.66 us (2%)
    pallas_call x1, Pallas kernels, compute(): pl.pallas_call(kernel, out_shape=(jax.ShapeDtypeStruct((SPEC, CELLS), F32...  9.51 us
    ppermute x1, waiting for transfers between devices, on_device(): after = lax.ppermute(lower, 'dev', down)  7.44 us
    unnamed x11, local copies, waits for them, and re-layouts  5.33 us
    ppermute x1, starting transfers between devices, on_device(): before = lax.ppermute(upper, 'dev', up)  4.95 us
    ppermute x1, starting transfers between devices, on_device(): after = lax.ppermute(lower, 'dev', down)  1.92 us
    ppermute x1, waiting for transfers between devices, on_device(): before = lax.ppermute(upper, 'dev', up)  0.89 us
    reshape x1, local copies, waits for them, and re-layouts, compute(): frequency.reshape(1, NR)  0.7 us
    reshape x1, local copies, waits for them, and re-layouts, compute(): barrier.reshape(1, NR)  0.7 us
  transfers between devices with their start and end apart: 2, of which 2 were waited for; matrix products, arithmetic and copies ran while one was open for 0% of the time, Pallas kernels for 0%

profile of v1, /device:TPU:126, one launch (start us, length us, event | category | flops | bytes accessed | tf_op | source)
XLA Modules:
  0.0 32.2 jit_solution(2711338246225406454)
XLA Ops:
  0.6 0.7 %reshape.14.frequency_ref = f32[1,1548]{1,0:T(1,128)S(1)} reshape(f32[1548]{0:T(1024)} %param.10) | data formatting | bytes 12384 | tf_op jit(solution)/shard_map/reshape | solution.py:399
  1.3 0.7 %reshape.15.barrier_ref = f32[1,1548]{1,0:T(1,128)S(1)} reshape(f32[1548]{0:T(1024)} %param.11) | data formatting | bytes 12384 | tf_op jit(solution)/shard_map/reshape | solution.py:400
  2.0 0.0 copy-start
  2.0 1.5 %copy-done = f32[258,1548]{1,0:T(8,128)S(1)} copy-done((f32[258,1548]{1,0:T(8,128)S(1)}, f32[258,1548]{1,0:T(8,128)}, u32[]{:S(2)}) %copy-start) | copy-done | bytes 1597560
  3.5 0.0 copy-start.1
  3.5 1.0 %copy-done.1 = f32[258,256]{1,0:T(8,128)S(1)} copy-done((f32[258,256]{1,0:T(8,128)S(1)}, f32[258,256]{1,0:T(8,128)}, u32[]{:S(2)}) %copy-start.1) | copy-done | bytes 264216
  4.5 0.0 copy-start.2
  4.5 0.7 %copy-done.2 = s32[2,1548]{1,0:T(2,128)S(1)} copy-done((s32[2,1548]{1,0:T(2,128)S(1)}, s32[2,1548]{1,0:T(2,128)}, u32[]{:S(2)}) %copy-start.2) | copy-done | bytes 12408
  5.2 0.0 copy-start.3
  5.2 0.7 %copy-done.3 = s32[256]{0:T(256)S(1)} copy-done((s32[256]{0:T(256)S(1)}, s32[256]{0:T(256)}, u32[]{:S(2)}) %copy-start.3) | copy-done | bytes 1048
  5.8 0.0 copy-start.4
  5.9 0.7 %copy-done.4 = s32[2,128]{1,0:T(2,128)S(1)} copy-done((s32[2,128]{1,0:T(2,128)S(1)}, s32[2,128]{1,0:T(2,128)}, u32[]{:S(2)}) %copy-start.4) | copy-done | bytes 1048
  6.5 9.5 %shard_map.86 = (f32[258,256]{1,0:T(8,128)}, f32[258,256]{1,0:T(8,128)S(1)}) custom-call(f32[258,256]{1,0:T(8,128)S(1)} %copy-done.1, s32[1,256]{1,0:T(1,128)S(1)} %bitcast.5, s32[2,1548]{1,0:T(2,128)S(1)} %copy-done.2, f32[1,1548]{1,0:T(1,128)S(1)} %reshape.14.frequency_ref, f32[1,1548]{1,0:T(1,128)S(1)} %reshape.15.barrier_ref, f32[258,1548]{1,0:T(8,128)S(1)} %copy-done, ...), custom_call_target="tpu_custom_call" | custom-call | flops 4000000000 | bytes 3000000 | tf_op jit(solution)/shard_map/pallas_call | solution.py:362
  16.1 4.9 %collective-permute-start = (f32[258,128]{1,0:T(8,128)S(1)}, f32[258,128]{1,0:T(8,128)S(1)}, u32[]{:S(2)}, u32[]{:S(2)}) collective-permute-start(f32[258,128]{1,0:T(8,128)S(1)} %get-tuple-element.10), channel_id=1, source_target_pairs={{0,1},{1,2},{2,3},{3,4},{4,5},{5,6},{6,7},{7,8},{8,9},{9,10},{10,1... | collective-permute-start | bytes 396296 | tf_op jit(solution)/shard_map/ppermute | solution.py:412
  21.0 1.9 %collective-permute-start.1 = (f32[258,128]{1,0:T(8,128)S(1)}, f32[258,128]{1,0:T(8,128)S(1)}, u32[]{:S(2)}, u32[]{:S(2)}) collective-permute-start(f32[258,128]{1,0:T(8,128)S(1)} %get-tuple-element.11), channel_id=1, source_target_pairs={{1,0},{2,1},{3,2},{4,3},{5,4},{6,5},{7,6},{8,7},{9,8},{10,9},{11,1... | collective-permute-start | bytes 396296 | tf_op jit(solution)/shard_map/ppermute | solution.py:413
  23.0 0.9 %collective-permute-done = f32[258,128]{1,0:T(8,128)S(1)} collective-permute-done((f32[258,128]{1,0:T(8,128)S(1)}, f32[258,128]{1,0:T(8,128)S(1)}, u32[]{:S(2)}, u32[]{:S(2)}) %collective-permute-start) | collective-permute-done | bytes 132128 | tf_op jit(solution)/shard_map/ppermute | solution.py:412
  23.8 7.4 %collective-permute-done.1 = f32[258,128]{1,0:T(8,128)S(1)} collective-permute-done((f32[258,128]{1,0:T(8,128)S(1)}, f32[258,128]{1,0:T(8,128)S(1)}, u32[]{:S(2)}, u32[]{:S(2)}) %collective-permute-start.1) | collective-permute-done | bytes 132128 | tf_op jit(solution)/shard_map/ppermute | solution.py:413
  31.4 0.8 %copy.9 = f32[258,2,128]{2,1,0:T(2,128)} copy(f32[258,2,128]{2,0,1:T(8,128)S(1)} %pad_maximum_fusion) | data formatting | bytes 528384
  (3 shorter events, 0.1 us)
Async XLA Ops:
  2.0 1.5 %copy-start = (f32[258,1548]{1,0:T(8,128)S(1)}, f32[258,1548]{1,0:T(8,128)}, u32[]{:S(2)}) copy-start(f32[258,1548]{1,0:T(8,128)} %stoich_ref.1) | copy-start | bytes 4792612
  3.5 1.0 %copy-start.1 = (f32[258,256]{1,0:T(8,128)S(1)}, f32[258,256]{1,0:T(8,128)}, u32[]{:S(2)}) copy-start(f32[258,256]{1,0:T(8,128)} %state_ref.1) | copy-start | bytes 792580
  4.5 0.7 %copy-start.2 = (s32[2,1548]{1,0:T(2,128)S(1)}, s32[2,1548]{1,0:T(2,128)}, u32[]{:S(2)}) copy-start(s32[2,1548]{1,0:T(2,128)} %reactants_ref.1) | copy-start | bytes 37156
  5.2 0.7 %copy-start.3 = (s32[256]{0:T(256)S(1)}, s32[256]{0:T(256)}, u32[]{:S(2)}) copy-start(s32[256]{0:T(256)} %param.8) | copy-start | bytes 3076
  5.8 0.7 %copy-start.4 = (s32[2,128]{1,0:T(2,128)S(1)}, s32[2,128]{1,0:T(2,128)}, u32[]{:S(2)}) copy-start(s32[2,128]{1,0:T(2,128)} %faces_ref.1) | copy-start | bytes 3076
  16.1 7.8 %collective-permute-start = (f32[258,128]{1,0:T(8,128)S(1)}, f32[258,128]{1,0:T(8,128)S(1)}, u32[]{:S(2)}, u32[]{:S(2)}) collective-permute-start(f32[258,128]{1,0:T(8,128)S(1)} %get-tuple-element.10), channel_id=1, source_target_pairs={{0,1},{1,2},{2,3},{3,4},{4,5},{5,6},{6,7},{7,8},{8,9},{9,10},{10,1... | collective-permute-start | bytes 396296 | tf_op jit(solution)/shard_map/ppermute | solution.py:412
  21.0 10.3 %collective-permute-start.1 = (f32[258,128]{1,0:T(8,128)S(1)}, f32[258,128]{1,0:T(8,128)S(1)}, u32[]{:S(2)}, u32[]{:S(2)}) collective-permute-start(f32[258,128]{1,0:T(8,128)S(1)} %get-tuple-element.11), channel_id=1, source_target_pairs={{1,0},{2,1},{3,2},{4,3},{5,4},{6,5},{7,6},{8,7},{9,8},{10,9},{11,1... | collective-permute-start | bytes 396296 | tf_op jit(solution)/shard_map/ppermute | solution.py:413

commit v2 on v1

--- a/solution.py
+++ b/solution.py
@@ -93,6 +93,15 @@
 
 
 def kernel(
+    state_hbm,
+    flags_hbm,
+    reactants_hbm,
+    frequency_hbm,
+    barrier_hbm,
+    stoich_hbm,
+    faces_hbm,
+    advanced_ref,
+    jump_ref,
     state_ref,
     flags_ref,
     reactants_ref,
@@ -100,8 +109,11 @@
     barrier_ref,
     stoich_ref,
     faces_ref,
-    advanced_ref,
-    face_ref,
+    in_sem,
+    face,
+    received,
+    send_sem,
+    recv_sem,
     rows,
     columns,
     s_hi,
@@ -122,12 +134,40 @@
     u1,
     u2,
 ):
+    me = lax.axis_index("dev")
+    count = lax.axis_size("dev")
+    up = lax.rem(me + 1, count)
+    down = lax.rem(me + count - 1, count)
+    barrier = pltpu.get_barrier_semaphore()
+    for other in (up, down):
+        pl.semaphore_signal(
+            barrier, inc=1, device_id={"dev": other}, device_id_type=pl.DeviceIdType.MESH
+        )
+    loads = [
+        pltpu.make_async_copy(src, dst, in_sem.at[k])
+        for k, (src, dst) in enumerate(
+            [
+                (frequency_hbm, frequency_ref),
+                (barrier_hbm, barrier_ref),
+                (reactants_hbm, reactants_ref),
+                (state_hbm, state_ref),
+                (stoich_hbm, stoich_ref),
+                (flags_hbm, flags_ref),
+                (faces_hbm, faces_ref),
+            ]
+        )
+    ]
+    for load in loads:
+        load.start()
+    for load in loads:
+        load.wait()
+
     rows[...] = jnp.zeros_like(rows)
     rows[:, 1536:] = jnp.where(
         lax.broadcasted_iota(jnp.int32, (8, 128), 0) >= 2, -1.0, 0.0
     )
-    rows[0:1, :NR] = frequency_ref[...]
-    rows[1:2, :NR] = barrier_ref[...]
+    rows[0:1, :NR] = frequency_ref[...].reshape(1, NR)
+    rows[1:2, :NR] = barrier_ref[...].reshape(1, NR)
     reactants = reactants_ref[...]
     lane = lax.broadcasted_iota(jnp.int32, (2, NR), 1)
     first = jnp.zeros((2, NR), jnp.int32)
@@ -340,7 +380,7 @@
                     for s, a, b, c in zip(base, one, two, three)
                 ],
             )
-            stiff = flags_ref[0:1, lanes] == 1
+            stiff = flags_ref[lanes].reshape(1, 128) == 1
             out = [
                 jnp.where(stiff, y + M[0] * a + M[1] * b + M[2] * c + M[3] * d, x)
                 for y, a, b, c, d, x in zip(
@@ -349,13 +389,33 @@
             ]
             for m in range(BS):
                 y_half[h, pl.ds(g * GROUP_STATE + m, GROUP, stride=BS), :] = out[m]
-        count = min(GROUP_STATE, SPEC - g * GROUP_STATE)
+        valid = min(GROUP_STATE, SPEC - g * GROUP_STATE)
         here = slice(g * GROUP_STATE, g * GROUP_STATE + GROUP_STATE)
-        real = slice(g * GROUP_STATE, g * GROUP_STATE + count)
+        real = slice(g * GROUP_STATE, g * GROUP_STATE + valid)
         done = jnp.concatenate([y_half[0, here, :], y_half[1, here, :]], axis=1)
-        advanced_ref[real, :] = done[:count]
-        face = sum(dot(part, hot) for part in split3(done))
-        face_ref[real, :] = face[:count]
+        advanced_ref[real, :] = done[:valid]
+        at_faces = sum(dot(part, hot) for part in split3(done))
+        for r in range(2):
+            face[r, here, :] = at_faces[:, r * FACES : (r + 1) * FACES]
+
+    pl.semaphore_wait(barrier, 2)
+    sends = [
+        pltpu.make_async_remote_copy(
+            src_ref=face.at[1 - r],
+            dst_ref=received.at[r],
+            send_sem=send_sem.at[r],
+            recv_sem=recv_sem.at[r],
+            device_id={"dev": other},
+            device_id_type=pl.DeviceIdType.MESH,
+        )
+        for r, other in ((0, up), (1, down))
+    ]
+    for send in sends:
+        send.start()
+    for r, (send, edge) in enumerate(zip(sends, (0, count - 1))):
+        send.wait()
+        inside = jnp.where(me == edge, 0.0, 1.0)
+        jump_ref[:, r, :] = jnp.where(inside > 0.5, received[r, :SPEC, :], 0.0) - face[r, :SPEC, :]
 
 
 def compute(state, flags, reactants, frequency, barrier, stoich, faces):
@@ -363,11 +423,23 @@
         kernel,
         out_shape=(
             jax.ShapeDtypeStruct((SPEC, CELLS), F32),
-            jax.ShapeDtypeStruct((SPEC, 2 * FACES), F32),
+            jax.ShapeDtypeStruct((SPEC, 2, FACES), F32),
         ),
-        in_specs=[pl.BlockSpec(memory_space=pltpu.VMEM)] * 7,
+        in_specs=[pl.BlockSpec(memory_space=pltpu.HBM)] * 7,
         out_specs=[pl.BlockSpec(memory_space=pltpu.VMEM)] * 2,
         scratch_shapes=[
+            pltpu.VMEM((SPEC, CELLS), F32),
+            pltpu.VMEM((CELLS,), jnp.int32),
+            pltpu.VMEM((2, NR), jnp.int32),
+            pltpu.VMEM((NR,), F32),
+            pltpu.VMEM((NR,), F32),
+            pltpu.VMEM((SPEC, NR), F32),
+            pltpu.VMEM((2, FACES), jnp.int32),
+            pltpu.SemaphoreType.DMA((7,)),
+            pltpu.VMEM((2, STATE_ROWS, FACES), F32),
+            pltpu.VMEM((2, STATE_ROWS, FACES), F32),
+            pltpu.SemaphoreType.DMA((2,)),
+            pltpu.SemaphoreType.DMA((2,)),
             pltpu.VMEM((8, RATE_ROWS), F32),
             pltpu.VMEM((RATE_ROWS, 8), F32),
             pltpu.VMEM((S_ROWS, RATE_ROWS), BF),
@@ -388,30 +460,23 @@
             pltpu.VMEM((STATE_ROWS, CELLS), F32),
             pltpu.VMEM((STATE_ROWS, CELLS), F32),
         ],
-        compiler_params=pltpu.CompilerParams(vmem_limit_bytes=48 * 1024 * 1024),
+        compiler_params=pltpu.CompilerParams(vmem_limit_bytes=60 * 1024 * 1024, collective_id=0, has_side_effects=True),
         cost_estimate=pl.CostEstimate(
             flops=4_000_000_000, bytes_accessed=3_000_000, transcendentals=400_000
         ),
     )(
         state,
-        flags.reshape(1, CELLS),
+        flags,
         reactants,
-        frequency.reshape(1, NR),
-        barrier.reshape(1, NR),
+        frequency,
+        barrier,
         stoich,
         faces,
     )
 
 
 def on_device(state, flags, reactants, frequency, barrier, stoich, faces):
-    advanced, face = compute(state, flags, reactants, frequency, barrier, stoich, faces)
-    lower, upper = face[:, :FACES], face[:, FACES:]
-    size = lax.axis_size("dev")
-    up = [(i, i + 1) for i in range(size - 1)]
-    down = [(i + 1, i) for i in range(size - 1)]
-    before = lax.ppermute(upper, "dev", up)
-    after = lax.ppermute(lower, "dev", down)
-    return advanced, jnp.stack([before - lower, after - upper], axis=1)
+    return compute(state, flags, reactants, frequency, barrier, stoich, faces)
 
 
 def solution(mesh):

time: 32.6 us -> 28 us (0.86)
  the two profiles are of different devices: /device:TPU:126 before, /device:TPU:1 now
where the time goes in v2:
time: 28 us; the launch traced here: 27.8 us
  Pallas kernels  23.8 us (85%)
  local copies, waits for them, and re-layouts  3.35 us (12%)
  between operations  0.64 us (2%)
    pallas_call x1, Pallas kernels, compute(): pl.pallas_call(kernel, out_shape=(jax.ShapeDtypeStruct((SPEC, CELLS), F32...  23.8 us
    unnamed x2, local copies, waits for them, and re-layouts  3.35 us

profile of v2, /device:TPU:1, one launch (start us, length us, event | category | flops | bytes accessed | tf_op | source)
XLA Modules:
  0.0 27.8 jit_solution(2841766693722414653)
XLA Ops:
  0.6 23.8 %shard_map.86 = (f32[258,256]{1,0:T(8,128)}, f32[258,2,128]{2,1,0:T(2,128)}) custom-call(f32[258,256]{1,0:T(8,128)} %state_hbm.1, s32[256]{0:T(256)} %flags_hbm.1, s32[2,1548]{1,0:T(2,128)} %reactants_hbm.1, f32[1548]{0:T(1024)} %frequency_hbm.1, f32[1548]{0:T(1024)} %barrier_hbm.1, f32[258,1548]{1,0:T(8,128)} %stoich_hbm.1, s32[2,128]{1,0:T(2,128)} %faces_hbm.1), custom_call_target="tpu_custom_call" | custom-call | flops 4000000000 | bytes 3000000 | tf_op jit(solution)/shard_map/pallas_call | solution.py:422
  24.4 1.7 %copy.11 = f32[258,256]{1,0:T(8,128)} copy(f32[258,256]{1,0:T(8,128)} %get-tuple-element.4) | data formatting | bytes 528384
  26.1 1.7 %copy.12 = f32[258,2,128]{2,1,0:T(2,128)} copy(f32[258,2,128]{2,1,0:T(2,128)} %get-tuple-element.5) | data formatting | bytes 528384

commit v3 on v2

--- a/solution.py
+++ b/solution.py
@@ -138,11 +138,23 @@
     count = lax.axis_size("dev")
     up = lax.rem(me + 1, count)
     down = lax.rem(me + count - 1, count)
+    has_up = me < count - 1
+    has_down = me > 0
     barrier = pltpu.get_barrier_semaphore()
-    for other in (up, down):
+
+    def greet(other):
         pl.semaphore_signal(
             barrier, inc=1, device_id={"dev": other}, device_id_type=pl.DeviceIdType.MESH
         )
+
+    @pl.when(has_up)
+    def _():
+        greet(up)
+
+    @pl.when(has_down)
+    def _():
+        greet(down)
+
     loads = [
         pltpu.make_async_copy(src, dst, in_sem.at[k])
         for k, (src, dst) in enumerate(
@@ -398,24 +410,37 @@
         for r in range(2):
             face[r, here, :] = at_faces[:, r * FACES : (r + 1) * FACES]
 
-    pl.semaphore_wait(barrier, 2)
-    sends = [
-        pltpu.make_async_remote_copy(
-            src_ref=face.at[1 - r],
-            dst_ref=received.at[r],
+    def neighbour(r, other):
+        return pltpu.make_async_remote_copy(
+            src_ref=face.at[r],
+            dst_ref=received.at[1 - r],
             send_sem=send_sem.at[r],
-            recv_sem=recv_sem.at[r],
+            recv_sem=recv_sem.at[1 - r],
             device_id={"dev": other},
             device_id_type=pl.DeviceIdType.MESH,
         )
-        for r, other in ((0, up), (1, down))
-    ]
-    for send in sends:
-        send.start()
-    for r, (send, edge) in enumerate(zip(sends, (0, count - 1))):
-        send.wait()
-        inside = jnp.where(me == edge, 0.0, 1.0)
-        jump_ref[:, r, :] = jnp.where(inside > 0.5, received[r, :SPEC, :], 0.0) - face[r, :SPEC, :]
+
+    pl.semaphore_wait(barrier, has_up.astype(jnp.int32) + has_down.astype(jnp.int32))
+
+    @pl.when(has_down)
+    def _():
+        neighbour(0, down).start()
+
+    @pl.when(has_up)
+    def _():
+        neighbour(1, up).start()
+
+    for r, there, other in ((0, has_down, down), (1, has_up, up)):
+
+        @pl.when(there)
+        def _(r=r, other=other):
+            neighbour(1 - r, other).wait_recv()
+            jump_ref[:, r, :] = received[r, :SPEC, :] - face[r, :SPEC, :]
+            neighbour(r, other).wait_send()
+
+        @pl.when(jnp.logical_not(there))
+        def _(r=r):
+            jump_ref[:, r, :] = 0.0 - face[r, :SPEC, :]
 
 
 def compute(state, flags, reactants, frequency, barrier, stoich, faces):
@@ -460,7 +485,7 @@
             pltpu.VMEM((STATE_ROWS, CELLS), F32),
             pltpu.VMEM((STATE_ROWS, CELLS), F32),
         ],
-        compiler_params=pltpu.CompilerParams(vmem_limit_bytes=60 * 1024 * 1024, collective_id=0, has_side_effects=True),
+        compiler_params=pltpu.CompilerParams(vmem_limit_bytes=32 * 1024 * 1024, collective_id=0, has_side_effects=True),
         cost_estimate=pl.CostEstimate(
             flops=4_000_000_000, bytes_accessed=3_000_000, transcendentals=400_000
         ),
@@ -476,7 +501,8 @@
 
 
 def on_device(state, flags, reactants, frequency, barrier, stoich, faces):
-    return compute(state, flags, reactants, frequency, barrier, stoich, faces)
+    args = [pltpu.with_memory_space_constraint(x, pltpu.HBM) for x in (state, flags, reactants, frequency, barrier, stoich, faces)]
+    return compute(*args)
 
 
 def solution(mesh):

time: 28 us -> 20.2 us (0.72)
  the two profiles are of different devices: /device:TPU:1 before, /device:TPU:200 now
where the time goes in v3:
time: 20.2 us; the launch traced here: 20.1 us
  Pallas kernels  18 us (89%)
  local copies, waits for them, and re-layouts  1.41 us (7%)
  between operations  0.64 us (3%)
    pallas_call x1, Pallas kernels, compute(): pl.pallas_call(kernel, out_shape=(jax.ShapeDtypeStruct((SPEC, CELLS), F32...  18 us
    unnamed x2, local copies, waits for them, and re-layouts  1.41 us

profile of v3, /device:TPU:200, one launch (start us, length us, event | category | flops | bytes accessed | tf_op | source)
XLA Modules:
  0.0 20.1 jit_solution(5635972614630776138)
XLA Ops:
  0.6 18.0 %shard_map.86 = (f32[258,256]{1,0:T(8,128)S(1)}, f32[258,2,128]{2,1,0:T(2,128)S(1)}) custom-call(f32[258,256]{1,0:T(8,128)} %state_hbm.1, s32[256]{0:T(256)} %flags_hbm.1, s32[2,1548]{1,0:T(2,128)} %reactants_hbm.1, f32[1548]{0:T(1024)} %frequency_hbm.1, f32[1548]{0:T(1024)} %barrier_hbm.1, f32[258,1548]{1,0:T(8,128)} %stoich_hbm.1, s32[2,128]{1,0:T(2,128)} %faces_hbm.1), custom_call_target="tpu_custom_call" | custom-call | flops 4000000000 | bytes 3000000 | tf_op jit(solution)/shard_map/pallas_call | solution.py:447
  18.6 0.7 %copy.11 = f32[258,256]{1,0:T(8,128)} copy(f32[258,256]{1,0:T(8,128)S(1)} %get-tuple-element.4) | data formatting | bytes 528384
  19.3 0.7 %copy.12 = f32[258,2,128]{2,1,0:T(2,128)} copy(f32[258,2,128]{2,1,0:T(2,128)S(1)} %get-tuple-element.5) | data formatting | bytes 528384

commit v4 on v3

v4 whole, which is shorter than its diff:
```python
import jax
import jax.numpy as jnp
from jax import lax
from jax.experimental import pallas as pl
from jax.experimental.pallas import tpu as pltpu
from jax.sharding import PartitionSpec as P

NB = 43
BS = 6
RPB = 36
SPEC = 258
NR = 1548
CELLS = 256
FACES = 128

TRIO = 3
TRIOS = 15
TRIO_STATE = TRIO * BS
TRIO_RATES = TRIO * RPB
TRIO_ROWS = 24
JAC_ROWS = BS * TRIO_ROWS
LONG = 8 * TRIO_STATE
STATE_ROWS = 2 * LONG + 8
RATE_ROWS = 1552
FAC_ROWS = 1664
S_ROWS = 272
MAIN = 1536
HALF = MAIN // 2

TIME_STEP = 0.01
GAMMA = 0.5
SCALED = TIME_STEP * GAMMA
A = (2.0, 1.867943637803922, 0.2344449711399156)
C = (
    -7.13761503641231,
    2.580708087951457,
    0.6515950076447975,
    -2.137148994382534,
    -0.3214669691237626,
    -0.6949742501781779,
)
M = (2.255570073418735, 0.2870493262186792, 0.435317943184018, 1.093502252409163)

BF = jnp.bfloat16
F32 = jnp.float32
I32 = jnp.int32
MESH = pl.DeviceIdType.MESH

ROW_GATHER = lax.GatherDimensionNumbers(
    offset_dims=(),
    collapsed_slice_dims=(0,),
    start_index_map=(0,),
    operand_batching_dims=(1,),
    start_indices_batching_dims=(1,),
)


def dot(a, b):
    return jnp.dot(a, b, preferred_element_type=F32)


def split2(x):
    hi = x.astype(BF)
    return hi, (x - hi.astype(F32)).astype(BF)


def split3(x):
    hi = x.astype(BF)
    rest = x - hi.astype(F32)
    mid = rest.astype(BF)
    return hi, mid, (rest - mid.astype(F32)).astype(BF)


def take_rows(x, index):
    return lax.gather(
        x,
        index[..., None],
        ROW_GATHER,
        slice_sizes=(1, 1),
        mode=lax.GatherScatterMode.PROMISE_IN_BOUNDS,
    )


def factor(e):
    for p in range(BS):
        inverse = 1.0 / e[p][p]
        e[p][p] = inverse
        for t in range(p + 1, BS):
            e[t][p] = e[t][p] * inverse
            for c in range(p + 1, BS):
                e[t][c] = e[t][c] - e[t][p] * e[p][c]
    return e


def solve(e, b):
    x = list(b)
    for t in range(BS):
        for c in range(t):
            x[t] = x[t] - e[t][c] * x[c]
    for t in reversed(range(BS)):
        for c in range(t + 1, BS):
            x[t] = x[t] - e[t][c] * x[c]
        x[t] = x[t] * e[t][t]
    return x


def both(a, b):
    return jnp.concatenate([a, b], axis=0)


def lanes(h):
    return slice(h * 128, (h + 1) * 128)


CHUNKS = [(r, s, h) for s in range(2) for h in range(2) for r in range(TRIO)]


def kernel(
    state_hbm,
    flags_hbm,
    reactants_hbm,
    frequency_hbm,
    barrier_hbm,
    stoich_hbm,
    faces_hbm,
    advanced_ref,
    jump_ref,
    state_ref,
    flags_ref,
    reactants_ref,
    frequency_ref,
    barrier_ref,
    stoich_ref,
    faces_ref,
    in_sem,
    face,
    received,
    send_sem,
    recv_sem,
    rows,
    columns,
    index,
    coef,
    y0,
    y,
    part,
    s_split,
    s_tail,
    tail,
    trio,
    r_hi,
    r_lo,
    fac,
    jac,
    lu,
    u1,
    u2,
    explicit,
):
    me = lax.axis_index("dev")
    count = lax.axis_size("dev")
    up = lax.rem(me + 1, count)
    down = lax.rem(me + count - 1, count)
    has_up = me < count - 1
    has_down = me > 0
    barrier = pltpu.get_barrier_semaphore()

    def greet(other):
        pl.semaphore_signal(barrier, inc=1, device_id={"dev": other}, device_id_type=MESH)

    @pl.when(has_up)
    def _():
        greet(up)

    @pl.when(has_down)
    def _():
        greet(down)

    loads = [
        pltpu.make_async_copy(src, dst, in_sem.at[k])
        for k, (src, dst) in enumerate(
            [
                (reactants_hbm, reactants_ref),
                (frequency_hbm, frequency_ref),
                (barrier_hbm, barrier_ref),
                (state_hbm, state_ref),
                (stoich_hbm, stoich_ref),
                (flags_hbm, flags_ref),
                (faces_hbm, faces_ref),
            ]
        )
    ]
    for load in loads:
        load.start()

    rows[...] = jnp.zeros_like(rows)
    tail[...] = jnp.zeros_like(tail)
    jac[:, TRIOS * JAC_ROWS :, :] = jnp.zeros((2, JAC_ROWS, 128), F32)
    y0[:, SPEC // 8 * 8 :, :] = jnp.zeros((2, STATE_ROWS - SPEC // 8 * 8, 128), F32)
    part[:, :, S_ROWS:, :] = jnp.zeros((2, 2, STATE_ROWS - S_ROWS, 128), F32)
    fac[:, RATE_ROWS:, :] = jnp.zeros((2, FAC_ROWS - RATE_ROWS, CELLS), BF)
    for load in loads:
        load.wait()

    reactants = reactants_ref[...]
    first = ((lax.broadcasted_iota(I32, (2, NR), 1) * 1821) >> 16) * BS
    rows[0:1, :NR] = frequency_ref[...].reshape(1, NR)
    rows[1:2, :NR] = barrier_ref[...].reshape(1, NR)
    rows[2:4, :NR] = (reactants - first).astype(F32)
    rows[4:6, :NR] = reactants.astype(F32)
    columns[...] = jnp.transpose(rows[...])

    for h in range(2):
        y0[h, :SPEC, :] = state_ref[:, lanes(h)]

    sub = lax.broadcasted_iota(I32, (8, 128), 0)

    def reactant(ref, h, at, want):
        one = at // RPB
        two = min((at + 7) // RPB, NB - 1)
        got = take_rows(ref[h, one * BS : one * BS + 8, :], want)
        if two != one:
            other = take_rows(ref[h, two * BS : two * BS + 8, :], want)
            got = jnp.where(sub < two * RPB - at, got, other)
        return got

    def put_rates(at, h, values):
        hi, lo = split2(both(*values))
        r_hi[at : at + 16, lanes(h)] = hi
        r_lo[at : at + 16, lanes(h)] = lo

    theta = 1.0 - 1.0 / state_ref[SPEC - 1 : SPEC, :]
    for at in range(0, RATE_ROWS, 16):
        wants, freq, ener = [], [], []
        for k in (at, at + 8):
            freq.append(jnp.broadcast_to(columns[k : k + 8, 0:1], (8, 128)))
            ener.append(jnp.broadcast_to(columns[k : k + 8, 1:2], (8, 128)))
            want = [
                jnp.broadcast_to(columns[k : k + 8, 2 + w : 3 + w], (8, 128)).astype(I32)
                for w in range(2)
            ]
            for w in range(2):
                index[w, k : k + 8, :] = want[w]
            wants.append(want)
        for h in range(2):
            one, two, rate = [], [], []
            for q, k in enumerate((at, at + 8)):
                c = freq[q] * jnp.exp(ener[q] * theta[:, lanes(h)])
                coef[h, k : k + 8, :] = c
                former = reactant(y0, h, k, wants[q][0])
                latter = reactant(y0, h, k, wants[q][1])
                one.append(c * latter)
                two.append(c * former)
                rate.append(one[-1] * former)
            fac[0, at : at + 16, lanes(h)] = both(*one).astype(BF)
            fac[1, at : at + 16, lanes(h)] = both(*two).astype(BF)
            put_rates(at, h, rate)

    for at in range(0, SPEC, 16):
        n = min(16, SPEC - at)
        x = stoich_ref[at : at + n, :MAIN]
        if n < 16:
            x = both(x, jnp.zeros((16 - n, MAIN), F32))
        hi, lo = split2(x)
        s_split[at : at + 16, :] = hi
        s_split[S_ROWS + at : S_ROWS + at + 16, :] = lo
    tail[:SPEC, : NR - MAIN] = stoich_ref[:, MAIN:]
    for at in range(0, S_ROWS, 16):
        x = tail[at : at + 16, :]
        hi = x.astype(BF).astype(F32)
        lo = x - hi
        s_tail[at : at + 16, :] = (hi + pltpu.roll(lo, 16, 1) + pltpu.roll(hi, 32, 1)).astype(BF)

    def source_term():
        for k in range(2):
            span = slice(k * HALF, (k + 1) * HALF)
            long = dot(s_split[:, span], r_hi[span, :])
            total = long[:S_ROWS] + long[S_ROWS:] + dot(s_split[:S_ROWS, span], r_lo[span, :])
            if k == 1:
                last = jnp.concatenate([r_hi[MAIN:, :], r_hi[MAIN:, :], r_lo[MAIN:, :]], axis=0)
                total = total + dot(s_tail[:, :48], last)
            for h in range(2):
                part[k, h, :S_ROWS, :] = total[:, lanes(h)]

    def rates():
        for at in range(0, RATE_ROWS, 16):
            wants = [[index[w, k : k + 8, :] for w in range(2)] for k in (at, at + 8)]
            for h in range(2):
                put_rates(
                    at,
                    h,
                    [
                        coef[h, k : k + 8, :]
                        * reactant(y, h, k, want[0])
                        * reactant(y, h, k, want[1])
                        for k, want in zip((at, at + 8), wants)
                    ],
                )

    source_term()

    shift = ((lax.broadcasted_iota(I32, (TRIO_ROWS, 1), 0) * 43) >> 8) * BS
    for t in range(TRIOS):
        start = t * TRIO_RATES // 16 * 16
        low = start // 128 * 128
        top = t * TRIO_STATE
        n = min(TRIO_STATE, SPEC - top)
        wide = min(256, NR - low)
        if wide < 256 or n < TRIO_STATE:
            trio[...] = jnp.zeros_like(trio)
        trio[:n, :wide] = stoich_ref[top : top + n, low : low + wide] * -SCALED
        x = trio[...]
        reacts = rows[:, low : low + 256]
        if start > low:
            x = pltpu.roll(x, 256 - (start - low), 1)
            reacts = pltpu.roll(reacts, 256 - (start - low), 1)
        x = x[:, :128]
        reacts = reacts[:, :128]
        sides = []
        for w in range(2):
            where = reacts[4 + w : 5 + w, :].astype(I32) - (shift + top)
            sides.append(
                jnp.concatenate([jnp.where(where == m, x, 0.0) for m in range(BS)], axis=0)
            )
        coupling = jnp.concatenate([side.astype(BF) for side in sides], axis=1)
        factors_here = both(fac[0, start : start + 128, :], fac[1, start : start + 128, :])
        block = dot(coupling, factors_here)
        for h in range(2):
            jac[h, t * JAC_ROWS : (t + 1) * JAC_ROWS, :] = block[:, lanes(h)]

    def state_rows(r, s, m):
        return pl.ds(s * LONG + r * BS + m, 8, stride=TRIO_STATE)

    def spread(ref, r, s, h):
        return [ref[h, state_rows(r, s, m), :] for m in range(BS)]

    def source(r, s, h):
        return [
            part[0, h, state_rows(r, s, m), :] + part[1, h, state_rows(r, s, m), :]
            for m in range(BS)
        ]

    def put_state(ref, r, s, h, values):
        for m in range(BS):
            ref[h, state_rows(r, s, m), :] = values[m]

    def keep(ref, k, values):
        for m in range(BS):
            ref[k, m] = values[m]

    def kept(ref, k):
        return [ref[k, m] for m in range(BS)]

    def factors(k):
        return [[lu[k, i, m] for m in range(BS)] for i in range(BS)]

    for k, (r, s, h) in enumerate(CHUNKS):
        e = [
            [
                jac[h, pl.ds(s * 8 * JAC_ROWS + m * TRIO_ROWS + r * BS + i, 8, stride=JAC_ROWS), :]
                for m in range(BS)
            ]
            for i in range(BS)
        ]
        for i in range(BS):
            e[i][i] = 1.0 + e[i][i]
        e = factor(e)
        for i in range(BS):
            for m in range(BS):
                lu[k, i, m] = e[i][m]
        rhs = source(r, s, h)
        x = solve(e, rhs)
        start = spread(y0, r, s, h)
        keep(u1, k, x)
        keep(explicit, k, [a + TIME_STEP * b for a, b in zip(start, rhs)])
        put_state(y, r, s, h, [a + (SCALED * A[0]) * b for a, b in zip(start, x)])

    rates()
    source_term()
    for k, (r, s, h) in enumerate(CHUNKS):
        one = kept(u1, k)
        x = solve(factors(k), [a + (GAMMA * C[0]) * b for a, b in zip(source(r, s, h), one)])
        keep(u2, k, x)
        put_state(
            y,
            r,
            s,
            h,
            [
                a + (SCALED * A[1]) * b + (SCALED * A[2]) * c
                for a, b, c in zip(spread(y0, r, s, h), one, x)
            ],
        )

    rates()
    source_term()

    spot = lax.broadcasted_iota(I32, (CELLS, FACES), 0)
    hot = jnp.concatenate([spot == faces_ref[0:1, :], spot == faces_ref[1:2, :]], axis=1)
    hot = hot.astype(F32).astype(BF)

    def neighbour(r, s, other):
        here = pl.ds(s * LONG, LONG)
        return pltpu.make_async_remote_copy(
            src_ref=face.at[r, here],
            dst_ref=received.at[1 - r, here],
            send_sem=send_sem.at[r, s],
            recv_sem=recv_sem.at[1 - r, s],
            device_id={"dev": other},
            device_id_type=MESH,
        )

    for s in range(2):
        for k, (r, s_k, h) in enumerate(CHUNKS):
            if s_k != s:
                continue
            e = factors(k)
            one = kept(u1, k)
            two = kept(u2, k)
            base = source(r, s, h)
            three = solve(
                e,
                [
                    z + (GAMMA * C[1]) * a + (GAMMA * C[2]) * b
                    for z, a, b in zip(base, one, two)
                ],
            )
            four = solve(
                e,
                [
                    z + (GAMMA * C[3]) * a + (GAMMA * C[4]) * b + (GAMMA * C[5]) * c
                    for z, a, b, c in zip(base, one, two, three)
                ],
            )
            stiff = flags_ref[lanes(h)].reshape(1, 128) == 1
            put_state(
                y,
                r,
                s,
                h,
                [
                    jnp.where(
                        stiff,
                        z
                        + (SCALED * M[0]) * a
                        + (SCALED * M[1]) * b
                        + (SCALED * M[2]) * c
                        + (SCALED * M[3]) * d,
                        x,
                    )
                    for z, a, b, c, d, x in zip(
                        spread(y0, r, s, h), one, two, three, four, kept(explicit, k)
                    )
                ],
            )
        here = slice(s * LONG, (s + 1) * LONG)
        n = min(LONG, SPEC - s * LONG)
        done = jnp.concatenate([y[0, here, :], y[1, here, :]], axis=1)
        advanced_ref[s * LONG : s * LONG + n, :] = done[:n]
        at_faces = sum(dot(p, hot) for p in split3(done))
        for r in range(2):
            face[r, here, :] = at_faces[:, r * FACES : (r + 1) * FACES]

        if s == 0:
            pl.semaphore_wait(barrier, has_up.astype(I32) + has_down.astype(I32))

        @pl.when(has_down)
        def _(s=s):
            neighbour(0, s, down).start()

        @pl.when(has_up)
        def _(s=s):
            neighbour(1, s, up).start()

    for r, there, other in ((0, has_down, down), (1, has_up, up)):

        @pl.when(there)
        def _(r=r, other=other):
            for s in range(2):
                neighbour(1 - r, s, other).wait_recv()
                here = slice(s * LONG, min(SPEC, (s + 1) * LONG))
                jump_ref[here, r, :] = received[r, here, :] - face[r, here, :]
            for s in range(2):
                neighbour(r, s, other).wait_send()

        @pl.when(jnp.logical_not(there))
        def _(r=r):
            jump_ref[:, r, :] = 0.0 - face[r, :SPEC, :]


def on_device(*args):
    args = [pltpu.with_memory_space_constraint(x, pltpu.HBM) for x in args]
    half = (2, STATE_ROWS, 128)
    chunks = len(CHUNKS)
    return pl.pallas_call(
        kernel,
        out_shape=(
            jax.ShapeDtypeStruct((SPEC, CELLS), F32),
            jax.ShapeDtypeStruct((SPEC, 2, FACES), F32),
        ),
        in_specs=[pl.BlockSpec(memory_space=pltpu.HBM)] * 7,
        out_specs=[pl.BlockSpec(memory_space=pltpu.VMEM)] * 2,
        scratch_shapes=[
            pltpu.VMEM((SPEC, CELLS), F32),
            pltpu.VMEM((CELLS,), I32),
            pltpu.VMEM((2, NR), I32),
            pltpu.VMEM((NR,), F32),
            pltpu.VMEM((NR,), F32),
            pltpu.VMEM((SPEC, NR), F32),
            pltpu.VMEM((2, FACES), I32),
            pltpu.SemaphoreType.DMA((7,)),
            pltpu.VMEM((2, 2 * LONG, FACES), F32),
            pltpu.VMEM((2, 2 * LONG, FACES), F32),
            pltpu.SemaphoreType.DMA((2, 2)),
            pltpu.SemaphoreType.DMA((2, 2)),
            pltpu.VMEM((8, FAC_ROWS), F32),
            pltpu.VMEM((FAC_ROWS, 8), F32),
            pltpu.VMEM((2, RATE_ROWS, 128), I32),
            pltpu.VMEM((2, RATE_ROWS, 128), F32),
            pltpu.VMEM(half, F32),
            pltpu.VMEM(half, F32),
            pltpu.VMEM((2,) + half, F32),
            pltpu.VMEM((2 * S_ROWS, MAIN), BF),
            pltpu.VMEM((S_ROWS, 128), BF),
            pltpu.VMEM((S_ROWS, 128), F32),
            pltpu.VMEM((TRIO_ROWS, 256), F32),
            pltpu.VMEM((RATE_ROWS, CELLS), BF),
            pltpu.VMEM((RATE_ROWS, CELLS), BF),
            pltpu.VMEM((2, FAC_ROWS, CELLS), BF),
            pltpu.VMEM((2, 16 * JAC_ROWS, 128), F32),
            pltpu.VMEM((chunks, BS, BS, 8, 128), F32),
            pltpu.VMEM((chunks, BS, 8, 128), F32),
            pltpu.VMEM((chunks, BS, 8, 128), F32),
            pltpu.VMEM((chunks, BS, 8, 128), F32),
        ],
        compiler_params=pltpu.CompilerParams(
            vmem_limit_bytes=32 * 1024 * 1024, collective_id=0, has_side_effects=True
        ),
        cost_estimate=pl.CostEstimate(
            flops=4_000_000_000, bytes_accessed=3_000_000, transcendentals=400_000
        ),
    )(*args)


def solution(mesh):
    cells = P(None, ("grp", "dev"))
    return jax.shard_map(
        on_device,
        mesh=mesh,
        in_specs=(cells, P(("grp", "dev")), P(), P(), P(), P(), cells),
        out_specs=(cells, P(None, None, ("grp", "dev"))),
        check_vma=False,
    )
```

time: 20.2 us -> 17.7 us (0.88)
  Pallas kernels: 18 us -> 15.5 us
    pallas_call x1, Pallas kernels: 18 us -> 15.5 us  [on_device(): pl.pallas_call(kernel, out_shape=(jax.ShapeDtypeStruct((SPEC, CELLS), F32...]
where the time goes in v4:
time: 17.7 us; the launch traced here: 17.5 us
  Pallas kernels  15.5 us (88%)
  local copies, waits for them, and re-layouts  1.41 us (8%)
  between operations  0.64 us (4%)
    pallas_call x1, Pallas kernels, on_device(): pl.pallas_call(kernel, out_shape=(jax.ShapeDtypeStruct((SPEC, CELLS), F32...  15.5 us
    unnamed x2, local copies, waits for them, and re-layouts  1.41 us

profile of v4, /device:TPU:200, one launch (start us, length us, event | category | flops | bytes accessed | tf_op | source)
XLA Modules:
  0.0 17.5 jit_solution(16634663178966121790)
XLA Ops:
  0.6 15.5 %shard_map.86 = (f32[258,256]{1,0:T(8,128)S(1)}, f32[258,2,128]{2,1,0:T(2,128)S(1)}) custom-call(f32[258,256]{1,0:T(8,128)} %state_hbm.1, s32[256]{0:T(256)} %flags_hbm.1, s32[2,1548]{1,0:T(2,128)} %reactants_hbm.1, f32[1548]{0:T(1024)} %frequency_hbm.1, f32[1548]{0:T(1024)} %barrier_hbm.1, f32[258,1548]{1,0:T(8,128)} %stoich_hbm.1, s32[2,128]{1,0:T(2,128)} %faces_hbm.1), custom_call_target="tpu_custom_call" | custom-call | flops 4000000000 | bytes 3000000 | tf_op jit(solution)/shard_map/pallas_call | solution.py:495
  16.1 0.7 %copy.11 = f32[258,256]{1,0:T(8,128)} copy(f32[258,256]{1,0:T(8,128)S(1)} %get-tuple-element.4) | data formatting | bytes 528384
  16.8 0.7 %copy.12 = f32[258,2,128]{2,1,0:T(2,128)} copy(f32[258,2,128]{2,1,0:T(2,128)S(1)} %get-tuple-element.5) | data formatting | bytes 528384

commit v5 on v4

--- a/solution.py
+++ b/solution.py
@@ -19,6 +19,7 @@
 TRIO_RATES = TRIO * RPB
 TRIO_ROWS = 24
 JAC_ROWS = BS * TRIO_ROWS
+PITCH = JAC_ROWS + 2
 LONG = 8 * TRIO_STATE
 STATE_ROWS = 2 * LONG + 8
 RATE_ROWS = 1552
@@ -26,6 +27,8 @@
 S_ROWS = 272
 MAIN = 1536
 HALF = MAIN // 2
+SPREAD = 144
+EARLY = 4 * SPREAD
 
 TIME_STEP = 0.01
 GAMMA = 0.5
@@ -55,6 +58,15 @@
 )
 
 
+LANE_GATHER = lax.GatherDimensionNumbers(
+    offset_dims=(),
+    collapsed_slice_dims=(1,),
+    start_index_map=(1,),
+    operand_batching_dims=(0,),
+    start_indices_batching_dims=(0,),
+)
+
+
 def dot(a, b):
     return jnp.dot(a, b, preferred_element_type=F32)
 
@@ -76,6 +88,16 @@
         x,
         index[..., None],
         ROW_GATHER,
+        slice_sizes=(1, 1),
+        mode=lax.GatherScatterMode.PROMISE_IN_BOUNDS,
+    )
+
+
+def take_lanes(x, index):
+    return lax.gather(
+        x,
+        index[..., None],
+        LANE_GATHER,
         slice_sizes=(1, 1),
         mode=lax.GatherScatterMode.PROMISE_IN_BOUNDS,
     )
@@ -139,6 +161,7 @@
     recv_sem,
     rows,
     columns,
+    whole,
     index,
     coef,
     y0,
@@ -195,20 +218,27 @@
 
     rows[...] = jnp.zeros_like(rows)
     tail[...] = jnp.zeros_like(tail)
-    jac[:, TRIOS * JAC_ROWS :, :] = jnp.zeros((2, JAC_ROWS, 128), F32)
+    jac[:, TRIOS * PITCH :, :] = jnp.zeros((2, PITCH, 128), F32)
     y0[:, SPEC // 8 * 8 :, :] = jnp.zeros((2, STATE_ROWS - SPEC // 8 * 8, 128), F32)
-    part[:, :, S_ROWS:, :] = jnp.zeros((2, 2, STATE_ROWS - S_ROWS, 128), F32)
+    part[:, :, :, S_ROWS:, :] = jnp.zeros((2, 4, 2, STATE_ROWS - S_ROWS, 128), F32)
     fac[:, RATE_ROWS:, :] = jnp.zeros((2, FAC_ROWS - RATE_ROWS, CELLS), BF)
-    for load in loads:
+    for load in loads[:3]:
         load.wait()
 
     reactants = reactants_ref[...]
     first = ((lax.broadcasted_iota(I32, (2, NR), 1) * 1821) >> 16) * BS
-    rows[0:1, :NR] = frequency_ref[...].reshape(1, NR)
-    rows[1:2, :NR] = barrier_ref[...].reshape(1, NR)
-    rows[2:4, :NR] = (reactants - first).astype(F32)
-    rows[4:6, :NR] = reactants.astype(F32)
-    columns[...] = jnp.transpose(rows[...])
+    for k, ref in ((0, frequency_ref), (3, barrier_ref)):
+        for q, piece in enumerate(split3(ref[...].reshape(1, NR))):
+            rows[k + q : k + q + 1, :NR] = piece.astype(F32)
+    rows[6:8, :NR] = (reactants - first).astype(F32)
+    whole[...] = jnp.zeros_like(whole)
+    whole[0:2, :NR] = reactants
+    columns[...] = jnp.transpose(rows[...]).astype(BF)
+    row = lax.broadcasted_iota(I32, (8, 512), 0)
+    col = lax.broadcasted_iota(I32, (8, 512), 1)
+    pick = (row >= 3).astype(I32) + (row >= 6).astype(I32) + (row >= 7).astype(I32)
+    pick = (pick == (col >> 7)).astype(F32).astype(BF)
+    loads[3].wait()
 
     for h in range(2):
         y0[h, :SPEC, :] = state_ref[:, lanes(h)]
@@ -230,15 +260,13 @@
         r_lo[at : at + 16, lanes(h)] = lo
 
     theta = 1.0 - 1.0 / state_ref[SPEC - 1 : SPEC, :]
-    for at in range(0, RATE_ROWS, 16):
+    def begin(at, wide):
         wants, freq, ener = [], [], []
         for k in (at, at + 8):
-            freq.append(jnp.broadcast_to(columns[k : k + 8, 0:1], (8, 128)))
-            ener.append(jnp.broadcast_to(columns[k : k + 8, 1:2], (8, 128)))
-            want = [
-                jnp.broadcast_to(columns[k : k + 8, 2 + w : 3 + w], (8, 128)).astype(I32)
-                for w in range(2)
-            ]
+            own = wide[k % SPREAD : k % SPREAD + 8, :]
+            freq.append(own[:, :128])
+            ener.append(own[:, 128:256])
+            want = [own[:, 256 + w * 128 : 384 + w * 128].astype(I32) for w in range(2)]
             for w in range(2):
                 index[w, k : k + 8, :] = want[w]
             wants.append(want)
@@ -256,61 +284,92 @@
             fac[1, at : at + 16, lanes(h)] = both(*two).astype(BF)
             put_rates(at, h, rate)
 
-    for at in range(0, SPEC, 16):
-        n = min(16, SPEC - at)
-        x = stoich_ref[at : at + n, :MAIN]
-        if n < 16:
-            x = both(x, jnp.zeros((16 - n, MAIN), F32))
-        hi, lo = split2(x)
-        s_split[at : at + 16, :] = hi
-        s_split[S_ROWS + at : S_ROWS + at + 16, :] = lo
-    tail[:SPEC, : NR - MAIN] = stoich_ref[:, MAIN:]
-    for at in range(0, S_ROWS, 16):
-        x = tail[at : at + 16, :]
-        hi = x.astype(BF).astype(F32)
-        lo = x - hi
-        s_tail[at : at + 16, :] = (hi + pltpu.roll(lo, 16, 1) + pltpu.roll(hi, 32, 1)).astype(BF)
-
-    def source_term():
-        for k in range(2):
-            span = slice(k * HALF, (k + 1) * HALF)
-            long = dot(s_split[:, span], r_hi[span, :])
-            total = long[:S_ROWS] + long[S_ROWS:] + dot(s_split[:S_ROWS, span], r_lo[span, :])
-            if k == 1:
-                last = jnp.concatenate([r_hi[MAIN:, :], r_hi[MAIN:, :], r_lo[MAIN:, :]], axis=0)
-                total = total + dot(s_tail[:, :48], last)
+    def split_stoichiometry(k):
+        span = slice(k * HALF, (k + 1) * HALF)
+        for at in range(0, SPEC, 16):
+            n = min(16, SPEC - at)
+            x = stoich_ref[at : at + n, span]
+            if n < 16:
+                x = both(x, jnp.zeros((16 - n, HALF), F32))
+            hi, lo = split2(x)
+            s_split[at : at + 16, span] = hi
+            s_split[S_ROWS + at : S_ROWS + at + 16, span] = lo
+
+    def split_tail():
+        tail[:SPEC, : NR - MAIN] = stoich_ref[:, MAIN:]
+        for at in range(0, S_ROWS, 16):
+            x = tail[at : at + 16, :]
+            hi = x.astype(BF).astype(F32)
+            lo = x - hi
+            s_tail[at : at + 16, :] = (
+                hi + pltpu.roll(lo, 16, 1) + pltpu.roll(hi, 32, 1)
+            ).astype(BF)
+
+    def source_part(stage, k):
+        low, mid, near, high = (k * HALF + q for q in (0, 512, 256, 768))
+        long = dot(s_split[:, low:mid], r_hi[low:mid, :])
+        one = long[:S_ROWS] + long[S_ROWS:] + dot(s_split[:S_ROWS, low:near], r_lo[low:near, :])
+        long = dot(s_split[:, mid:high], r_hi[mid:high, :])
+        two = long[:S_ROWS] + long[S_ROWS:] + dot(s_split[:S_ROWS, near:high], r_lo[near:high, :])
+        if k == 1:
+            last = jnp.concatenate([r_hi[MAIN:, :], r_hi[MAIN:, :], r_lo[MAIN:, :]], axis=0)
+            two = two + dot(s_tail[:, :48], last)
+        for q, total in enumerate((one, two)):
             for h in range(2):
-                part[k, h, :S_ROWS, :] = total[:, lanes(h)]
-
-    def rates():
-        for at in range(0, RATE_ROWS, 16):
-            wants = [[index[w, k : k + 8, :] for w in range(2)] for k in (at, at + 8)]
-            for h in range(2):
-                put_rates(
-                    at,
-                    h,
-                    [
-                        coef[h, k : k + 8, :]
-                        * reactant(y, h, k, want[0])
-                        * reactant(y, h, k, want[1])
-                        for k, want in zip((at, at + 8), wants)
-                    ],
-                )
-
-    source_term()
+                part[stage % 2, 2 * k + q, h, :S_ROWS, :] = total[:, lanes(h)]
+
+    def again(at):
+        wants = [[index[w, k : k + 8, :] for w in range(2)] for k in (at, at + 8)]
+        for h in range(2):
+            put_rates(
+                at,
+                h,
+                [
+                    coef[h, k : k + 8, :] * reactant(y, h, k, want[0]) * reactant(y, h, k, want[1])
+                    for k, want in zip((at, at + 8), wants)
+                ],
+            )
+
+    def state_rows(r, s, m):
+        return pl.ds(s * LONG + r * BS + m, 8, stride=TRIO_STATE)
+
+    def spread(ref, r, s, h):
+        return [ref[h, state_rows(r, s, m), :] for m in range(BS)]
+
+    def source(stage, r, s, h):
+        own = part.at[stage % 2]
+        return [
+            (own[0, h, state_rows(r, s, m), :] + own[1, h, state_rows(r, s, m), :])
+            + (own[2, h, state_rows(r, s, m), :] + own[3, h, state_rows(r, s, m), :])
+            for m in range(BS)
+        ]
+
+    def put_state(ref, r, s, h, values):
+        for m in range(BS):
+            ref[h, state_rows(r, s, m), :] = values[m]
+
+    def keep(ref, k, values):
+        for m in range(BS):
+            ref[k, m] = values[m]
+
+    def kept(ref, k):
+        return [ref[k, m] for m in range(BS)]
+
+    def factors(k):
+        return [[lu[k, i, m] for m in range(BS)] for i in range(BS)]
 
     shift = ((lax.broadcasted_iota(I32, (TRIO_ROWS, 1), 0) * 43) >> 8) * BS
-    for t in range(TRIOS):
+    def jacobian(t):
         start = t * TRIO_RATES // 16 * 16
         low = start // 128 * 128
         top = t * TRIO_STATE
         n = min(TRIO_STATE, SPEC - top)
         wide = min(256, NR - low)
         if wide < 256 or n < TRIO_STATE:
-            trio[...] = jnp.zeros_like(trio)
-        trio[:n, :wide] = stoich_ref[top : top + n, low : low + wide] * -SCALED
-        x = trio[...]
-        reacts = rows[:, low : low + 256]
+            trio[t] = jnp.zeros((TRIO_ROWS, 256), F32)
+        trio[t, :n, :wide] = stoich_ref[top : top + n, low : low + wide] * -SCALED
+        x = trio[t]
+        reacts = whole[:, low : low + 256]
         if start > low:
             x = pltpu.roll(x, 256 - (start - low), 1)
             reacts = pltpu.roll(reacts, 256 - (start - low), 1)
@@ -318,7 +377,7 @@
         reacts = reacts[:, :128]
         sides = []
         for w in range(2):
-            where = reacts[4 + w : 5 + w, :].astype(I32) - (shift + top)
+            where = reacts[w : w + 1, :] - (shift + top)
             sides.append(
                 jnp.concatenate([jnp.where(where == m, x, 0.0) for m in range(BS)], axis=0)
             )
@@ -326,60 +385,37 @@
         factors_here = both(fac[0, start : start + 128, :], fac[1, start : start + 128, :])
         block = dot(coupling, factors_here)
         for h in range(2):
-            jac[h, t * JAC_ROWS : (t + 1) * JAC_ROWS, :] = block[:, lanes(h)]
-
-    def state_rows(r, s, m):
-        return pl.ds(s * LONG + r * BS + m, 8, stride=TRIO_STATE)
-
-    def spread(ref, r, s, h):
-        return [ref[h, state_rows(r, s, m), :] for m in range(BS)]
-
-    def source(r, s, h):
-        return [
-            part[0, h, state_rows(r, s, m), :] + part[1, h, state_rows(r, s, m), :]
-            for m in range(BS)
-        ]
-
-    def put_state(ref, r, s, h, values):
-        for m in range(BS):
-            ref[h, state_rows(r, s, m), :] = values[m]
-
-    def keep(ref, k, values):
-        for m in range(BS):
-            ref[k, m] = values[m]
-
-    def kept(ref, k):
-        return [ref[k, m] for m in range(BS)]
-
-    def factors(k):
-        return [[lu[k, i, m] for m in range(BS)] for i in range(BS)]
-
-    for k, (r, s, h) in enumerate(CHUNKS):
-        e = [
-            [
-                jac[h, pl.ds(s * 8 * JAC_ROWS + m * TRIO_ROWS + r * BS + i, 8, stride=JAC_ROWS), :]
-                for m in range(BS)
+            jac[h, t * PITCH : t * PITCH + JAC_ROWS, :] = block[:, lanes(h)]
+
+    def eliminate(s):
+        for k, (r, s_k, h) in enumerate(CHUNKS):
+            if s_k != s:
+                continue
+            e = [
+                [
+                    jac[h, pl.ds(s * 8 * PITCH + m * TRIO_ROWS + r * BS + i, 8, stride=PITCH), :]
+                    for m in range(BS)
+                ]
+                for i in range(BS)
             ]
-            for i in range(BS)
-        ]
-        for i in range(BS):
-            e[i][i] = 1.0 + e[i][i]
-        e = factor(e)
-        for i in range(BS):
-            for m in range(BS):
-                lu[k, i, m] = e[i][m]
-        rhs = source(r, s, h)
-        x = solve(e, rhs)
+            for i in range(BS):
+                e[i][i] = 1.0 + e[i][i]
+            e = factor(e)
+            for i in range(BS):
+                for m in range(BS):
+                    lu[k, i, m] = e[i][m]
+
+    def first_stage(k, r, s, h):
+        rhs = source(0, r, s, h)
+        x = solve(factors(k), rhs)
         start = spread(y0, r, s, h)
         keep(u1, k, x)
         keep(explicit, k, [a + TIME_STEP * b for a, b in zip(start, rhs)])
         put_state(y, r, s, h, [a + (SCALED * A[0]) * b for a, b in zip(start, x)])
 
-    rates()
-    source_term()
-    for k, (r, s, h) in enumerate(CHUNKS):
+    def second_stage(k, r, s, h):
         one = kept(u1, k)
-        x = solve(factors(k), [a + (GAMMA * C[0]) * b for a, b in zip(source(r, s, h), one)])
+        x = solve(factors(k), [a + (GAMMA * C[0]) * b for a, b in zip(source(1, r, s, h), one)])
         keep(u2, k, x)
         put_state(
             y,
@@ -392,12 +428,41 @@
             ],
         )
 
-    rates()
-    source_term()
-
-    spot = lax.broadcasted_iota(I32, (CELLS, FACES), 0)
-    hot = jnp.concatenate([spot == faces_ref[0:1, :], spot == faces_ref[1:2, :]], axis=1)
-    hot = hot.astype(F32).astype(BF)
+    def next_source(stage, step):
+        for half in range(2):
+            for k, (r, s, h) in enumerate(CHUNKS):
+                if s == half:
+                    step(k, r, s, h)
+            for at in range(half * HALF, HALF if half == 0 else RATE_ROWS, 16):
+                again(at)
+            source_part(stage, half)
+
+    for at in range(0, RATE_ROWS, 16):
+        if at % SPREAD == 0:
+            wide = dot(columns[at : min(at + SPREAD, RATE_ROWS), :], pick)
+        if at == EARLY:
+            for load in loads[4:]:
+                load.wait()
+        begin(at, wide)
+        if at + 16 == HALF:
+            split_stoichiometry(0)
+            source_part(0, 0)
+    split_stoichiometry(1)
+    split_tail()
+    for t in range(8):
+        jacobian(t)
+    source_part(0, 1)
+    for t in range(8, TRIOS):
+        jacobian(t)
+    eliminate(0)
+    eliminate(1)
+
+    next_source(1, first_stage)
+    next_source(2, second_stage)
+
+    cells = [jnp.broadcast_to(faces_ref[r : r + 1, :], (8, FACES)) for r in range(2)]
+    near = [c < 128 for c in cells]
+    cells = [c & 127 for c in cells]
 
     def neighbour(r, s, other):
         here = pl.ds(s * LONG, LONG)
@@ -417,7 +482,7 @@
             e = factors(k)
             one = kept(u1, k)
             two = kept(u2, k)
-            base = source(r, s, h)
+            base = source(2, r, s, h)
             three = solve(
                 e,
                 [
@@ -425,10 +490,13 @@
                     for z, a, b in zip(base, one, two)
                 ],
             )
-            four = solve(
+            rest = solve(
                 e,
                 [
-                    z + (GAMMA * C[3]) * a + (GAMMA * C[4]) * b + (GAMMA * C[5]) * c
+                    (M[2] + M[3]) * z
+                    + (GAMMA * (M[2] * C[1] + M[3] * C[3])) * a
+                    + (GAMMA * (M[2] * C[2] + M[3] * C[4])) * b
+                    + (GAMMA * M[3] * C[5]) * c
                     for z, a, b, c in zip(base, one, two, three)
                 ],
             )
@@ -441,15 +509,11 @@
                 [
                     jnp.where(
                         stiff,
-                        z
-                        + (SCALED * M[0]) * a
-                        + (SCALED * M[1]) * b
-                        + (SCALED * M[2]) * c
-                        + (SCALED * M[3]) * d,
+                        z + (SCALED * M[0]) * a + (SCALED * M[1]) * b + SCALED * d,
                         x,
                     )
-                    for z, a, b, c, d, x in zip(
-                        spread(y0, r, s, h), one, two, three, four, kept(explicit, k)
+                    for z, a, b, d, x in zip(
+                        spread(y0, r, s, h), one, two, rest, kept(explicit, k)
                     )
                 ],
             )
@@ -457,9 +521,12 @@
         n = min(LONG, SPEC - s * LONG)
         done = jnp.concatenate([y[0, here, :], y[1, here, :]], axis=1)
         advanced_ref[s * LONG : s * LONG + n, :] = done[:n]
-        at_faces = sum(dot(p, hot) for p in split3(done))
-        for r in range(2):
-            face[r, here, :] = at_faces[:, r * FACES : (r + 1) * FACES]
+        for at in range(s * LONG, (s + 1) * LONG, 8):
+            halves = [y[h, at : at + 8, :] for h in range(2)]
+            for r in range(2):
+                face[r, at : at + 8, :] = jnp.where(
+                    near[r], take_lanes(halves[0], cells[r]), take_lanes(halves[1], cells[r])
+                )
 
         if s == 0:
             pl.semaphore_wait(barrier, has_up.astype(I32) + has_down.astype(I32))
@@ -478,25 +545,38 @@
         def _(r=r, other=other):
             for s in range(2):
                 neighbour(1 - r, s, other).wait_recv()
-                here = slice(s * LONG, min(SPEC, (s + 1) * LONG))
-                jump_ref[here, r, :] = received[r, here, :] - face[r, here, :]
+                n = min(SPEC - s * LONG, LONG)
+                here = slice(s * LONG, s * LONG + n)
+                jump_ref[r, here, :] = received[r, here, :] - face[r, here, :]
             for s in range(2):
                 neighbour(r, s, other).wait_send()
 
         @pl.when(jnp.logical_not(there))
         def _(r=r):
-            jump_ref[:, r, :] = 0.0 - face[r, :SPEC, :]
+            jump_ref[r] = 0.0 - face[r, :SPEC, :]
+
+
+def write(advanced, jump, advanced_hbm, jump_hbm, sem):
+    copies = [
+        pltpu.make_async_copy(advanced, advanced_hbm, sem.at[0]),
+        pltpu.make_async_copy(jump.at[0], jump_hbm.at[:, 0, :], sem.at[1]),
+        pltpu.make_async_copy(jump.at[1], jump_hbm.at[:, 1, :], sem.at[2]),
+    ]
+    for copy in copies:
+        copy.start()
+    for copy in copies:
+        copy.wait()
 
 
 def on_device(*args):
     args = [pltpu.with_memory_space_constraint(x, pltpu.HBM) for x in args]
     half = (2, STATE_ROWS, 128)
     chunks = len(CHUNKS)
-    return pl.pallas_call(
+    advanced, jump = pl.pallas_call(
         kernel,
         out_shape=(
             jax.ShapeDtypeStruct((SPEC, CELLS), F32),
-            jax.ShapeDtypeStruct((SPEC, 2, FACES), F32),
+            jax.ShapeDtypeStruct((2, SPEC, FACES), F32),
         ),
         in_specs=[pl.BlockSpec(memory_space=pltpu.HBM)] * 7,
         out_specs=[pl.BlockSpec(memory_space=pltpu.VMEM)] * 2,
@@ -514,20 +594,21 @@
             pltpu.SemaphoreType.DMA((2, 2)),
             pltpu.SemaphoreType.DMA((2, 2)),
             pltpu.VMEM((8, FAC_ROWS), F32),
-            pltpu.VMEM((FAC_ROWS, 8), F32),
+            pltpu.VMEM((FAC_ROWS, 8), BF),
+            pltpu.VMEM((8, FAC_ROWS), I32),
             pltpu.VMEM((2, RATE_ROWS, 128), I32),
             pltpu.VMEM((2, RATE_ROWS, 128), F32),
             pltpu.VMEM(half, F32),
             pltpu.VMEM(half, F32),
-            pltpu.VMEM((2,) + half, F32),
+            pltpu.VMEM((2, 4) + half, F32),
             pltpu.VMEM((2 * S_ROWS, MAIN), BF),
             pltpu.VMEM((S_ROWS, 128), BF),
             pltpu.VMEM((S_ROWS, 128), F32),
-            pltpu.VMEM((TRIO_ROWS, 256), F32),
+            pltpu.VMEM((TRIOS, TRIO_ROWS, 256), F32),
             pltpu.VMEM((RATE_ROWS, CELLS), BF),
             pltpu.VMEM((RATE_ROWS, CELLS), BF),
             pltpu.VMEM((2, FAC_ROWS, CELLS), BF),
-            pltpu.VMEM((2, 16 * JAC_ROWS, 128), F32),
+            pltpu.VMEM((2, 16 * PITCH, 128), F32),
             pltpu.VMEM((chunks, BS, BS, 8, 128), F32),
             pltpu.VMEM((chunks, BS, 8, 128), F32),
             pltpu.VMEM((chunks, BS, 8, 128), F32),
@@ -540,6 +621,17 @@
             flops=4_000_000_000, bytes_accessed=3_000_000, transcendentals=400_000
         ),
     )(*args)
+    return pl.pallas_call(
+        write,
+        out_shape=(
+            jax.ShapeDtypeStruct((SPEC, CELLS), F32),
+            jax.ShapeDtypeStruct((SPEC, 2, FACES), F32),
+        ),
+        in_specs=[pl.BlockSpec(memory_space=pltpu.VMEM)] * 2,
+        out_specs=[pl.BlockSpec(memory_space=pltpu.HBM)] * 2,
+        scratch_shapes=[pltpu.SemaphoreType.DMA((3,))],
+        compiler_params=pltpu.CompilerParams(vmem_limit_bytes=32 * 1024 * 1024),
+    )(advanced, jump)
 
 
 def solution(mesh):

time: 17.7 us -> 15.6 us (0.88)
  local copies, waits for them, and re-layouts: 1.41 us -> 0 us
  Pallas kernels: 15.5 us -> 14.8 us
    pallas_call x1, Pallas kernels: 15.5 us -> 14 us  [on_device(): pl.pallas_call(kernel, out_shape=(jax.ShapeDtypeStruct((SPEC, CELLS), F32...]
    unnamed x2 -> x0, local copies, waits for them, and re-layouts: 1.41 us -> none
    pallas_call x0 -> x1, Pallas kernels: none -> 0.82 us  [on_device(): pl.pallas_call(write, out_shape=(jax.ShapeDtypeStruct((SPEC, CELLS), F32)...]
where the time goes in v5:
time: 15.6 us; the launch traced here: 15.4 us
  Pallas kernels  14.8 us (95%)
  between operations  0.64 us (4%)
    pallas_call x1, Pallas kernels, on_device(): pl.pallas_call(kernel, out_shape=(jax.ShapeDtypeStruct((SPEC, CELLS), F32...  14 us
    pallas_call x1, Pallas kernels, on_device(): pl.pallas_call(write, out_shape=(jax.ShapeDtypeStruct((SPEC, CELLS), F32)...  0.82 us

profile of v5, /device:TPU:200, one launch (start us, length us, event | category | flops | bytes accessed | tf_op | source)
XLA Modules:
  0.0 15.4 jit_solution(12372434087114401384)
XLA Ops:
  0.6 14.0 %shard_map.86 = (f32[258,256]{1,0:T(8,128)S(1)}, f32[2,258,128]{2,1,0:T(8,128)S(1)}) custom-call(f32[258,256]{1,0:T(8,128)} %state_hbm.1, s32[256]{0:T(256)} %flags_hbm.1, s32[2,1548]{1,0:T(2,128)} %reactants_hbm.1, f32[1548]{0:T(1024)} %frequency_hbm.1, f32[1548]{0:T(1024)} %barrier_hbm.1, f32[258,1548]{1,0:T(8,128)} %stoich_hbm.1, s32[2,128]{1,0:T(2,128)} %faces_hbm.1), custom_call_target="tpu_custom_call" | custom-call | flops 4000000000 | bytes 3000000 | tf_op jit(solution)/shard_map/pallas_call | solution.py:575
  14.6 0.8 %shard_map.87 = (f32[258,256]{1,0:T(8,128)}, f32[258,2,128]{2,1,0:T(2,128)}) custom-call(f32[258,256]{1,0:T(8,128)S(1)} %get-tuple-element.4.advanced, f32[2,258,128]{2,1,0:T(8,128)S(1)} %get-tuple-element.5.jump), custom_call_target="tpu_custom_call" | custom-call | tf_op jit(solution)/shard_map/pallas_call | solution.py:624

commit v6 on v5

--- a/solution.py
+++ b/solution.py
@@ -27,6 +27,7 @@
 S_ROWS = 272
 MAIN = 1536
 HALF = MAIN // 2
+FACE_ROWS = 264
 SPREAD = 144
 EARLY = 4 * SPREAD
 
@@ -162,6 +163,7 @@
     rows,
     columns,
     whole,
+    spots,
     index,
     coef,
     y0,
@@ -230,14 +232,14 @@
     for k, ref in ((0, frequency_ref), (3, barrier_ref)):
         for q, piece in enumerate(split3(ref[...].reshape(1, NR))):
             rows[k + q : k + q + 1, :NR] = piece.astype(F32)
-    rows[6:8, :NR] = (reactants - first).astype(F32)
     whole[...] = jnp.zeros_like(whole)
     whole[0:2, :NR] = reactants
+    whole[2:4, :NR] = reactants - first
+    spots[...] = jnp.transpose(whole[...])
     columns[...] = jnp.transpose(rows[...]).astype(BF)
-    row = lax.broadcasted_iota(I32, (8, 512), 0)
-    col = lax.broadcasted_iota(I32, (8, 512), 1)
-    pick = (row >= 3).astype(I32) + (row >= 6).astype(I32) + (row >= 7).astype(I32)
-    pick = (pick == (col >> 7)).astype(F32).astype(BF)
+    row = lax.broadcasted_iota(I32, (8, 256), 0)
+    col = lax.broadcasted_iota(I32, (8, 256), 1)
+    pick = ((row >= 3) == (col >= 128)).astype(F32).astype(BF)
     loads[3].wait()
 
     for h in range(2):
@@ -266,7 +268,9 @@
             own = wide[k % SPREAD : k % SPREAD + 8, :]
             freq.append(own[:, :128])
             ener.append(own[:, 128:256])
-            want = [own[:, 256 + w * 128 : 384 + w * 128].astype(I32) for w in range(2)]
+            want = [
+                jnp.broadcast_to(spots[k : k + 8, 2 + w : 3 + w], (8, 128)) for w in range(2)
+            ]
             for w in range(2):
                 index[w, k : k + 8, :] = want[w]
             wants.append(want)
@@ -305,18 +309,27 @@
                 hi + pltpu.roll(lo, 16, 1) + pltpu.roll(hi, 32, 1)
             ).astype(BF)
 
-    def source_part(stage, k):
+    def source_part(stage, k, top=0, end=S_ROWS):
         low, mid, near, high = (k * HALF + q for q in (0, 512, 256, 768))
-        long = dot(s_split[:, low:mid], r_hi[low:mid, :])
-        one = long[:S_ROWS] + long[S_ROWS:] + dot(s_split[:S_ROWS, low:near], r_lo[low:near, :])
-        long = dot(s_split[:, mid:high], r_hi[mid:high, :])
-        two = long[:S_ROWS] + long[S_ROWS:] + dot(s_split[:S_ROWS, near:high], r_lo[near:high, :])
+        n = end - top
+
+        def stacked(span):
+            hi = s_split[top:end, span]
+            lo = s_split[S_ROWS + top : S_ROWS + end, span]
+            long = dot(both(hi, lo), r_hi[span, :])
+            return long[:n] + long[n:]
+
+        def corrected(span):
+            return dot(s_split[top:end, span], r_lo[span, :])
+
+        one = stacked(slice(low, mid)) + corrected(slice(low, near))
+        two = stacked(slice(mid, high)) + corrected(slice(near, high))
         if k == 1:
             last = jnp.concatenate([r_hi[MAIN:, :], r_hi[MAIN:, :], r_lo[MAIN:, :]], axis=0)
-            two = two + dot(s_tail[:, :48], last)
+            two = two + dot(s_tail[top:end, :48], last)
         for q, total in enumerate((one, two)):
             for h in range(2):
-                part[stage % 2, 2 * k + q, h, :S_ROWS, :] = total[:, lanes(h)]
+                part[stage % 2, 2 * k + q, h, top:end, :] = total[:, lanes(h)]
 
     def again(at):
         wants = [[index[w, k : k + 8, :] for w in range(2)] for k in (at, at + 8)]
@@ -435,7 +448,10 @@
                     step(k, r, s, h)
             for at in range(half * HALF, HALF if half == 0 else RATE_ROWS, 16):
                 again(at)
-            source_part(stage, half)
+            if stage == 2 and half == 1:
+                source_part(stage, half, 0, LONG)
+            else:
+                source_part(stage, half)
 
     for at in range(0, RATE_ROWS, 16):
         if at % SPREAD == 0:
@@ -465,7 +481,7 @@
     cells = [c & 127 for c in cells]
 
     def neighbour(r, s, other):
-        here = pl.ds(s * LONG, LONG)
+        here = pl.ds(s * LONG, LONG if s == 0 else FACE_ROWS - LONG)
         return pltpu.make_async_remote_copy(
             src_ref=face.at[r, here],
             dst_ref=received.at[1 - r, here],
@@ -476,6 +492,8 @@
         )
 
     for s in range(2):
+        if s == 1:
+            source_part(2, 1, LONG, S_ROWS)
         for k, (r, s_k, h) in enumerate(CHUNKS):
             if s_k != s:
                 continue
@@ -521,7 +539,7 @@
         n = min(LONG, SPEC - s * LONG)
         done = jnp.concatenate([y[0, here, :], y[1, here, :]], axis=1)
         advanced_ref[s * LONG : s * LONG + n, :] = done[:n]
-        for at in range(s * LONG, (s + 1) * LONG, 8):
+        for at in range(s * LONG, LONG if s == 0 else FACE_ROWS, 8):
             halves = [y[h, at : at + 8, :] for h in range(2)]
             for r in range(2):
                 face[r, at : at + 8, :] = jnp.where(
@@ -589,13 +607,14 @@
             pltpu.VMEM((SPEC, NR), F32),
             pltpu.VMEM((2, FACES), I32),
             pltpu.SemaphoreType.DMA((7,)),
-            pltpu.VMEM((2, 2 * LONG, FACES), F32),
-            pltpu.VMEM((2, 2 * LONG, FACES), F32),
+            pltpu.VMEM((2, FACE_ROWS, FACES), F32),
+            pltpu.VMEM((2, FACE_ROWS, FACES), F32),
             pltpu.SemaphoreType.DMA((2, 2)),
             pltpu.SemaphoreType.DMA((2, 2)),
             pltpu.VMEM((8, FAC_ROWS), F32),
             pltpu.VMEM((FAC_ROWS, 8), BF),
             pltpu.VMEM((8, FAC_ROWS), I32),
+            pltpu.VMEM((FAC_ROWS, 8), I32),
             pltpu.VMEM((2, RATE_ROWS, 128), I32),
             pltpu.VMEM((2, RATE_ROWS, 128), F32),
             pltpu.VMEM(half, F32),

time: 15.6 us -> 15.3 us (0.981)
  Pallas kernels: 14.8 us -> 14.5 us
    pallas_call x1, Pallas kernels: 14 us -> 13.7 us  [on_device(): pl.pallas_call(kernel, out_shape=(jax.ShapeDtypeStruct((SPEC, CELLS), F32...]
where the time goes in v6:
time: 15.3 us; the launch traced here: 15.1 us
  Pallas kernels  14.5 us (95%)
  between operations  0.64 us (4%)
    pallas_call x1, Pallas kernels, on_device(): pl.pallas_call(kernel, out_shape=(jax.ShapeDtypeStruct((SPEC, CELLS), F32...  13.7 us
    pallas_call x1, Pallas kernels, on_device(): pl.pallas_call(write, out_shape=(jax.ShapeDtypeStruct((SPEC, CELLS), F32)...  0.82 us

profile of v6, /device:TPU:200, one launch (start us, length us, event | category | flops | bytes accessed | tf_op | source)
XLA Modules:
  0.0 15.1 jit_solution(9706100906629146091)
XLA Ops:
  0.6 13.7 %shard_map.86 = (f32[258,256]{1,0:T(8,128)S(1)}, f32[2,258,128]{2,1,0:T(8,128)S(1)}) custom-call(f32[258,256]{1,0:T(8,128)} %state_hbm.1, s32[256]{0:T(256)} %flags_hbm.1, s32[2,1548]{1,0:T(2,128)} %reactants_hbm.1, f32[1548]{0:T(1024)} %frequency_hbm.1, f32[1548]{0:T(1024)} %barrier_hbm.1, f32[258,1548]{1,0:T(8,128)} %stoich_hbm.1, s32[2,128]{1,0:T(2,128)} %faces_hbm.1), custom_call_target="tpu_custom_call" | custom-call | flops 4000000000 | bytes 3000000 | tf_op jit(solution)/shard_map/pallas_call | solution.py:593
  14.3 0.8 %shard_map.87 = (f32[258,256]{1,0:T(8,128)}, f32[258,2,128]{2,1,0:T(2,128)}) custom-call(f32[258,256]{1,0:T(8,128)S(1)} %get-tuple-element.4.advanced, f32[2,258,128]{2,1,0:T(8,128)S(1)} %get-tuple-element.5.jump), custom_call_target="tpu_custom_call" | custom-call | tf_op jit(solution)/shard_map/pallas_call | solution.py:643

commit v7 on v6

--- a/solution.py
+++ b/solution.py
@@ -186,21 +186,6 @@
     count = lax.axis_size("dev")
     up = lax.rem(me + 1, count)
     down = lax.rem(me + count - 1, count)
-    has_up = me < count - 1
-    has_down = me > 0
-    barrier = pltpu.get_barrier_semaphore()
-
-    def greet(other):
-        pl.semaphore_signal(barrier, inc=1, device_id={"dev": other}, device_id_type=MESH)
-
-    @pl.when(has_up)
-    def _():
-        greet(up)
-
-    @pl.when(has_down)
-    def _():
-        greet(down)
-
     loads = [
         pltpu.make_async_copy(src, dst, in_sem.at[k])
         for k, (src, dst) in enumerate(
@@ -218,6 +203,21 @@
     for load in loads:
         load.start()
 
+    has_up = me < count - 1
+    has_down = me > 0
+    barrier = pltpu.get_barrier_semaphore()
+
+    def greet(other):
+        pl.semaphore_signal(barrier, inc=1, device_id={"dev": other}, device_id_type=MESH)
+
+    @pl.when(has_up)
+    def _():
+        greet(up)
+
+    @pl.when(has_down)
+    def _():
+        greet(down)
+
     rows[...] = jnp.zeros_like(rows)
     tail[...] = jnp.zeros_like(tail)
     jac[:, TRIOS * PITCH :, :] = jnp.zeros((2, PITCH, 128), F32)
@@ -272,7 +272,7 @@
                 jnp.broadcast_to(spots[k : k + 8, 2 + w : 3 + w], (8, 128)) for w in range(2)
             ]
             for w in range(2):
-                index[w, k : k + 8, :] = want[w]
+                index[w, k : k + 8, :] = want[w] - sub
             wants.append(want)
         for h in range(2):
             one, two, rate = [], [], []
@@ -332,7 +332,7 @@
                 part[stage % 2, 2 * k + q, h, top:end, :] = total[:, lanes(h)]
 
     def again(at):
-        wants = [[index[w, k : k + 8, :] for w in range(2)] for k in (at, at + 8)]
+        wants = [[index[w, k : k + 8, :] + sub for w in range(2)] for k in (at, at + 8)]
         for h in range(2):
             put_rates(
                 at,
@@ -481,7 +481,7 @@
     cells = [c & 127 for c in cells]
 
     def neighbour(r, s, other):
-        here = pl.ds(s * LONG, LONG if s == 0 else FACE_ROWS - LONG)
+        here = pl.ds(s * LONG, LONG if s == 0 else SPEC - LONG)
         return pltpu.make_async_remote_copy(
             src_ref=face.at[r, here],
             dst_ref=received.at[1 - r, here],

time: 15.3 us -> 15.2 us (level)
  no operation moved by 1% of the time
where the time goes in v7:
time: 15.2 us; the launch traced here: 15 us
  Pallas kernels  14.4 us (95%)
  between operations  0.64 us (4%)
    pallas_call x1, Pallas kernels, on_device(): pl.pallas_call(kernel, out_shape=(jax.ShapeDtypeStruct((SPEC, CELLS), F32...  13.6 us
    pallas_call x1, Pallas kernels, on_device(): pl.pallas_call(write, out_shape=(jax.ShapeDtypeStruct((SPEC, CELLS), F32)...  0.82 us

profile of v7, /device:TPU:200, one launch (start us, length us, event | category | flops | bytes accessed | tf_op | source)
XLA Modules:
  0.0 15.0 jit_solution(7910852224523493964)
XLA Ops:
  0.6 13.6 %shard_map.86 = (f32[258,256]{1,0:T(8,128)S(1)}, f32[2,258,128]{2,1,0:T(8,128)S(1)}) custom-call(f32[258,256]{1,0:T(8,128)} %state_hbm.1, s32[256]{0:T(256)} %flags_hbm.1, s32[2,1548]{1,0:T(2,128)} %reactants_hbm.1, f32[1548]{0:T(1024)} %frequency_hbm.1, f32[1548]{0:T(1024)} %barrier_hbm.1, f32[258,1548]{1,0:T(8,128)} %stoich_hbm.1, s32[2,128]{1,0:T(2,128)} %faces_hbm.1), custom_call_target="tpu_custom_call" | custom-call | flops 4000000000 | bytes 3000000 | tf_op jit(solution)/shard_map/pallas_call | solution.py:593
  14.2 0.8 %shard_map.87 = (f32[258,256]{1,0:T(8,128)}, f32[258,2,128]{2,1,0:T(2,128)}) custom-call(f32[258,256]{1,0:T(8,128)S(1)} %get-tuple-element.4.advanced, f32[2,258,128]{2,1,0:T(8,128)S(1)} %get-tuple-element.5.jump), custom_call_target="tpu_custom_call" | custom-call | tf_op jit(solution)/shard_map/pallas_call | solution.py:643
